TPU v7x, 512 devices: a whole 4x8x8 slice. The times are simulated.
512 devices in a mesh: pool: 4 (over x), seq: 16 (over z, core), tp: 8 (over y).
Axes of the slice: x: 4, y: 8, z: 8, core: 2. Of those that a mesh axis runs over, the one named last changes fastest.
Arguments:
- queries: bfloat16 [64, 256, 8192], P(('pool', 'seq'), 'tp')
- stretch_kv: bfloat16 [64, 256, 8, 256], P(('pool', 'seq'), 'tp')
- pool_kv: bfloat16 [1024, 128, 8, 256], P(('pool', 'seq'), None, 'tp'), may hold values from -6 to 6
- prefix_blocks: int32 [64], replicated, may hold values from 24 to 48
- block_owner: int32 [64, 48], replicated, may hold values from 0 to 63, as said below
- block_slot: int32 [64, 48], replicated, may hold values from 0 to 15
Outputs:
- attended: bfloat16 [64, 256, 8192], P(('pool', 'seq'), 'tp')
Inputs may be any that keep to these rules, and one draw needn't show every extreme that they name: `block_owner`: among the first prefix_blocks[r] entries of row r no owner is named more than 1 times, and some request names one owner exactly 1 times.
All inputs are finite; a program needn't handle non-finite values.
Results may differ from a plain program's by a relative error of at most 0.005.
Values may be sent and summed in bfloat16 or wider, within the bound.
No kernel may reach another device: no remote copies, remote signals or barrier semaphores. Data moves between devices by JAX's collectives and lax.ppermute only.
A program may use at most 64 MiB of HBM per device.

v0:
```python
import math

import jax
import jax.numpy as jnp
from jax import lax
from jax.sharding import PartitionSpec as P

QH = 64
KVH = 8


MASKED_SCORE = -1e30


def local(queries, stretch_kv, pool_kv, prefix_blocks, block_owner, block_slot):
    tensor_count = lax.axis_size("tp")
    owner_count = lax.axis_size(("pool", "seq"))
    myself = lax.axis_index(("pool", "seq"))
    tok_local = queries.shape[1]
    stretch_len = tok_local * tensor_count
    block_len = pool_kv.shape[1]
    kv_local = pool_kv.shape[2]
    pair_width = pool_kv.shape[3]
    head_dim = pair_width // 2
    max_blocks = block_owner.shape[1]
    capacity = (max_blocks + owner_count - 1) // owner_count
    group_size = QH // KVH
    score_scale = 1.0 / math.sqrt(head_dim)
    q_parts = queries[0].reshape(tok_local, tensor_count, -1)
    kv_parts = stretch_kv[0]
    q_heads, kv_heads = (
        lax.all_to_all(q_parts, "tp", split_axis=1, concat_axis=0, tiled=True),
        lax.all_to_all(kv_parts, "tp", split_axis=1, concat_axis=0, tiled=True),
    )
    q_heads = q_heads.reshape(stretch_len, kv_local, group_size, head_dim)
    position = jnp.arange(max_blocks, dtype=jnp.int32)
    live_all = position[None, :] < prefix_blocks[:, None]
    owned = (block_owner == myself) & live_all
    owned_int = owned.astype(jnp.int32)
    owned_rank = jnp.cumsum(owned_int, axis=1) - owned_int
    slot_pick = (
        owned_rank[:, :, None] == jnp.arange(capacity, dtype=jnp.int32)[None, None, :]
    ) & owned[:, :, None]
    picked = jnp.sum(jnp.where(slot_pick, block_slot[:, :, None], 0), axis=1)
    outgoing = jnp.take(pool_kv, picked.reshape(-1), axis=0)
    outgoing = outgoing.reshape(owner_count, capacity, block_len, kv_local, pair_width)
    arrived = lax.all_to_all(outgoing, ("pool", "seq"), split_axis=0, concat_axis=0, tiled=True)
    arrived = arrived.reshape(owner_count * capacity, block_len, kv_local, pair_width)
    own_row = lax.dynamic_index_in_dim(block_owner, myself, 0, keepdims=False)
    own_len = lax.dynamic_index_in_dim(prefix_blocks, myself, 0, keepdims=False)
    own_live = position < own_len
    earlier = (
        (own_row[None, :] == own_row[:, None])
        & (position[None, :] < position[:, None])
        & own_live[None, :]
    )
    own_rank = jnp.sum(earlier.astype(jnp.int32), axis=1)
    source = jnp.where(own_live, own_row * capacity + own_rank, 0)
    prefix = jnp.take(arrived, source, axis=0).reshape(max_blocks * block_len, kv_local, pair_width)

    def attend(carried, key_block, usable):
        run_max, run_total, run_acc = carried
        scores = (
            jnp.einsum(
                "tkgd,skd->tkgs",
                q_heads,
                key_block[..., :head_dim],
                preferred_element_type=jnp.float32,
            )
            * score_scale
        )
        key_mask = usable[:, None, None, :]
        scores = jnp.where(key_mask, scores, MASKED_SCORE)
        new_max = jnp.maximum(run_max, jnp.max(scores, axis=-1))
        weights = jnp.where(key_mask, jnp.exp(scores - new_max[..., None]), 0.0)
        shrink = jnp.exp(run_max - new_max)
        run_total = run_total * shrink + jnp.sum(weights, axis=-1)
        run_acc = run_acc * shrink[..., None] + jnp.einsum(
            "tkgs,skd->tkgd",
            weights.astype(jnp.bfloat16),
            key_block[..., head_dim:],
            preferred_element_type=jnp.float32,
        )
        return (new_max, run_total, run_acc)

    per_step = max(1, 512 // block_len)
    while max_blocks % per_step:
        per_step -= 1
    step_keys = per_step * block_len
    step_total = max_blocks // per_step

    def prefix_step(step_index, carried):
        key_block = lax.dynamic_slice_in_dim(prefix, step_index * step_keys, step_keys, 0)
        key_position = step_index * step_keys + jnp.arange(step_keys, dtype=jnp.int32)
        usable = (key_position < own_len * block_len)[None, :]
        return attend(carried, key_block, usable)

    row_shape = (stretch_len, kv_local, group_size)
    initial = (
        jnp.full(row_shape, MASKED_SCORE, jnp.float32),
        jnp.zeros(row_shape, jnp.float32),
        jnp.zeros(row_shape + (head_dim,), jnp.float32),
    )
    carried = lax.fori_loop(0, step_total, prefix_step, initial)
    token = jnp.arange(stretch_len, dtype=jnp.int32)
    causal = token[None, :] <= token[:, None]
    run_max, run_total, run_acc = attend(carried, kv_heads, causal)
    output = (run_acc / run_total[..., None]).astype(jnp.bfloat16)
    output = output.reshape(tensor_count, tok_local, kv_local * group_size * head_dim)
    return lax.all_to_all(output, "tp", split_axis=0, concat_axis=2, tiled=True)


def solution(mesh):
    return jax.shard_map(
        local,
        mesh=mesh,
        in_specs=(
            P(("pool", "seq"), "tp", None),
            P(("pool", "seq"), "tp", None, None),
            P(("pool", "seq"), None, "tp", None),
            P(),
            P(),
            P(),
        ),
        out_specs=P(("pool", "seq"), "tp", None),
        check_vma=False,
    )
```

profile of v0, /device:TPU:7, one launch (start us, length us, event | category | flops | bytes accessed | tf_op | source)
XLA Modules:
  0.0 301.0 jit_solution(10284832305214173958)
XLA Ops:
  0.0 1.7 copy.74
  1.7 6.8 %all-to-all-start.2 = ((bf16[32,8,256]{2,0,1:T(8,128)(2,1)}), bf16[32,8,256]{2,0,1:T(8,128)(2,1)S(1)}, u32[]{:S(2)}, u32[]{:S(2)}) async-start(bf16[32,8,256]{2,0,1:T(8,128)(2,1)} %bitcast.191), calls=%async_computation.2 | async-start | bytes 262144 | tf_op jit(solution)/shard_map/all_to_all | solution.py:33
  8.5 0.8 copy.51
  9.3 0.8 copy.52
  10.1 1.3 copy.66
  11.5 1.1 copy.53
  12.5 0.7 fusion.50
  13.6 2.6 all-to-all-done.2
  16.2 4.0 %all-to-all-start.1 = ((bf16[32,8,1024]{2,0,1:T(8,128)(2,1)}), bf16[32,8,1024]{2,0,1:T(8,128)(2,1)S(1)}, u32[]{:S(2)}, u32[]{:S(2)}) async-start(bf16[32,8,1024]{2,0,1:T(8,128)(2,1)} %copy.53), calls=%async_computation.1 | async-start | bytes 1048576 | tf_op jit(solution)/shard_map/all_to_all | solution.py:32
  20.3 2.8 gather_fusion
  23.1 4.6 %bitcast_select_fusion.1 = bf16[64,1,128,1,256]{4,2,3,1,0:T(8,128)(2,1)} fusion(bf16[64,128,256]{2,1,0:T(8,128)(2,1)} %gather_fusion, pred[64]{0:T(512)(128)(4,1)S(1)} %compare_and_fusion), kind=kLoop, calls=%fused_computation.31 | loop fusion | flops 2097152 | bytes 8388672 | tf_op jit(solution)/shard_map/jit(_take)/select_n | solution.py:45
  27.7 8.5 %all-to-all-done.1 = bf16[32,8,1024]{2,0,1:T(8,128)(2,1)S(1)} async-done(((bf16[32,8,1024]{2,0,1:T(8,128)(2,1)}), bf16[32,8,1024]{2,0,1:T(8,128)(2,1)S(1)}, u32[]{:S(2)}, u32[]{:S(2)}) %all-to-all-start.1) | async-done | bytes 524320 | tf_op jit(solution)/shard_map/all_to_all | solution.py:32
  36.2 16.4 %all-to-all-start = ((bf16[64,1,128,1,256]{4,2,3,1,0:T(8,128)(2,1)}), bf16[64,1,128,1,256]{4,2,3,1,0:T(8,128)(2,1)}, u32[]{:S(2)}, u32[]{:S(2)}) async-start(bf16[64,1,128,1,256]{4,2,3,1,0:T(8,128)(2,1)} %bitcast_select_fusion.1), calls=%async_computation | async-start | bytes 8388608 | tf_op jit(solution)/shard_map/all_to_all | solution.py:47
  52.6 0.6 dynamic_slice.17
  53.9 0.6 iota_compare_fusion.3
  54.7 0.6 fusion.46
  55.4 0.6 compare_and_fusion.1
  56.2 1.8 fusion.23
  58.0 90.4 %all-to-all-done = bf16[64,1,128,1,256]{4,2,3,1,0:T(8,128)(2,1)} async-done(((bf16[64,1,128,1,256]{4,2,3,1,0:T(8,128)(2,1)}), bf16[64,1,128,1,256]{4,2,3,1,0:T(8,128)(2,1)}, u32[]{:S(2)}, u32[]{:S(2)}) %all-to-all-start) | async-done | bytes 4194336 | tf_op jit(solution)/shard_map/all_to_all | solution.py:47
  148.3 4.8 %gather_fusion.1 = bf16[48,128,256]{2,1,0:T(8,128)(2,1)} fusion(bf16[64,128,256]{2,1,0:T(8,128)(2,1)} %bitcast.6, s32[1024]{0:T(1024)S(1)} %pad_clamp_fusion), kind=kCustom, calls=%fused_computation.1 | custom fusion | bytes 6291648 | tf_op jit(solution)/shard_map/jit(_take)/gather | solution.py:59
  153.1 4.9 %bitcast_select_fusion.2 = bf16[6144,1,256]{2,0,1:T(8,128)(2,1)} fusion(bf16[48,128,256]{2,1,0:T(8,128)(2,1)} %gather_fusion.1, pred[6144]{0:T(1024)(128)(4,1)S(1)} %broadcast_bitcast_fusion), kind=kLoop, calls=%fused_computation.32 | loop fusion | flops 1572864 | bytes 6297600 | tf_op jit(solution)/shard_map/jit(_take)/select_n | solution.py:59
  158.0 117.0 %while.20 = (s32[]{:T(128)}, f32[256,1,8]{0,2,1:T(8,128)S(1)}, f32[256,1,8]{0,2,1:T(8,128)S(1)}, f32[256,1,8,128]{0,3,2,1:T(8,128)}, s32[]{:T(128)}, /*index=5*/...) while((s32[]{:T(128)}, f32[256,1,8]{0,2,1:T(8,128)S(1)}, ...), condition=%wide.region_6.7_spmd.clone, body=%wide.region_3.6_spmd.clone.sunk | while | flops 551302144 | bytes 32377576 | solution.py:104
  158.0 3.6 %bitcast_reduce_fusion.2 = (f32[256,8]{0,1:T(8,128)S(1)}, f32[512,256,8]{1,0,2:T(8,128)}) fusion(pred[512]{0:T(512)(128)(4,1)S(1)} %add_compare_fusion.2, bf16[256,1,8,128]{3,0,2,1:T(8,128)(2,1)S(1)} %get-tuple-element.337, bf16[6144,1,256]{2,0,1:T(8,128)(2,1)} %get-tuple-element.336, s32[]{:T(128)S(6)} %select_n.218), kind=kOutput, calls=%fused_computation.3.clone.1 | convolution fusion | flops 271579136 | bytes 4858372 | tf_op jit(solution)/shard_map/while/body/eval_jaxpr/tkgd,skd->tkgs/dot_general | solution.py:64
  161.6 4.7 %fusion.59 = f32[256,1,8,128]{0,3,2,1:T(8,128)} fusion(f32[512,256,8]{1,0,2:T(8,128)} %get-tuple-element.305, f32[256,8]{0,1:T(8,128)S(1)} %bitcast.223, pred[512]{0:T(512)(128)(4,1)S(1)} %add_compare_fusion.2, f32[256,1,8,128]{0,3,2,1:T(8,128)} %get-tuple-element.322, f32[256,8]{0,1:T(8,128)S(1)} %get-tuple-element.306, pred[]{:T(512)S(6)} %compare.3, ...), kind=kOutput, calls=%fused_computation.14.clone.1 | convolution fusion | flops 274464768 | bytes 6439945 | tf_op jit(solution)/shard_map/while/body/eval_jaxpr/tkgs,skd->tkgd/dot_general | solution.py:78
  166.2 1.2 fusion.58
  167.5 3.6 %bitcast_reduce_fusion.2 = (f32[256,8]{0,1:T(8,128)S(1)}, f32[512,256,8]{1,0,2:T(8,128)}) fusion(pred[512]{0:T(512)(128)(4,1)S(1)} %add_compare_fusion.2, bf16[256,1,8,128]{3,0,2,1:T(8,128)(2,1)S(1)} %get-tuple-element.337, bf16[6144,1,256]{2,0,1:T(8,128)(2,1)} %get-tuple-element.336, s32[]{:T(128)S(6)} %select_n.218), kind=kOutput, calls=%fused_computation.3.clone.1 | convolution fusion | flops 271579136 | bytes 4858372 | tf_op jit(solution)/shard_map/while/body/eval_jaxpr/tkgd,skd->tkgs/dot_general | solution.py:64
  171.0 5.0 %fusion.59 = f32[256,1,8,128]{0,3,2,1:T(8,128)} fusion(f32[512,256,8]{1,0,2:T(8,128)} %get-tuple-element.305, f32[256,8]{0,1:T(8,128)S(1)} %bitcast.223, pred[512]{0:T(512)(128)(4,1)S(1)} %add_compare_fusion.2, f32[256,1,8,128]{0,3,2,1:T(8,128)} %get-tuple-element.322, f32[256,8]{0,1:T(8,128)S(1)} %get-tuple-element.306, pred[]{:T(512)S(6)} %compare.3, ...), kind=kOutput, calls=%fused_computation.14.clone.1 | convolution fusion | flops 274464768 | bytes 6439945 | tf_op jit(solution)/shard_map/while/body/eval_jaxpr/tkgs,skd->tkgd/dot_general | solution.py:78
  176.0 1.2 fusion.58
  177.2 3.6 %bitcast_reduce_fusion.2 = (f32[256,8]{0,1:T(8,128)S(1)}, f32[512,256,8]{1,0,2:T(8,128)}) fusion(pred[512]{0:T(512)(128)(4,1)S(1)} %add_compare_fusion.2, bf16[256,1,8,128]{3,0,2,1:T(8,128)(2,1)S(1)} %get-tuple-element.337, bf16[6144,1,256]{2,0,1:T(8,128)(2,1)} %get-tuple-element.336, s32[]{:T(128)S(6)} %select_n.218), kind=kOutput, calls=%fused_computation.3.clone.1 | convolution fusion | flops 271579136 | bytes 4858372 | tf_op jit(solution)/shard_map/while/body/eval_jaxpr/tkgd,skd->tkgs/dot_general | solution.py:64
  180.8 5.0 %fusion.59 = f32[256,1,8,128]{0,3,2,1:T(8,128)} fusion(f32[512,256,8]{1,0,2:T(8,128)} %get-tuple-element.305, f32[256,8]{0,1:T(8,128)S(1)} %bitcast.223, pred[512]{0:T(512)(128)(4,1)S(1)} %add_compare_fusion.2, f32[256,1,8,128]{0,3,2,1:T(8,128)} %get-tuple-element.322, f32[256,8]{0,1:T(8,128)S(1)} %get-tuple-element.306, pred[]{:T(512)S(6)} %compare.3, ...), kind=kOutput, calls=%fused_computation.14.clone.1 | convolution fusion | flops 274464768 | bytes 6439945 | tf_op jit(solution)/shard_map/while/body/eval_jaxpr/tkgs,skd->tkgd/dot_general | solution.py:78
  185.8 1.2 fusion.58
  187.0 3.6 %bitcast_reduce_fusion.2 = (f32[256,8]{0,1:T(8,128)S(1)}, f32[512,256,8]{1,0,2:T(8,128)}) fusion(pred[512]{0:T(512)(128)(4,1)S(1)} %add_compare_fusion.2, bf16[256,1,8,128]{3,0,2,1:T(8,128)(2,1)S(1)} %get-tuple-element.337, bf16[6144,1,256]{2,0,1:T(8,128)(2,1)} %get-tuple-element.336, s32[]{:T(128)S(6)} %select_n.218), kind=kOutput, calls=%fused_computation.3.clone.1 | convolution fusion | flops 271579136 | bytes 4858372 | tf_op jit(solution)/shard_map/while/body/eval_jaxpr/tkgd,skd->tkgs/dot_general | solution.py:64
  190.6 5.0 %fusion.59 = f32[256,1,8,128]{0,3,2,1:T(8,128)} fusion(f32[512,256,8]{1,0,2:T(8,128)} %get-tuple-element.305, f32[256,8]{0,1:T(8,128)S(1)} %bitcast.223, pred[512]{0:T(512)(128)(4,1)S(1)} %add_compare_fusion.2, f32[256,1,8,128]{0,3,2,1:T(8,128)} %get-tuple-element.322, f32[256,8]{0,1:T(8,128)S(1)} %get-tuple-element.306, pred[]{:T(512)S(6)} %compare.3, ...), kind=kOutput, calls=%fused_computation.14.clone.1 | convolution fusion | flops 274464768 | bytes 6439945 | tf_op jit(solution)/shard_map/while/body/eval_jaxpr/tkgs,skd->tkgd/dot_general | solution.py:78
  195.6 1.2 fusion.58
  196.8 3.6 %bitcast_reduce_fusion.2 = (f32[256,8]{0,1:T(8,128)S(1)}, f32[512,256,8]{1,0,2:T(8,128)}) fusion(pred[512]{0:T(512)(128)(4,1)S(1)} %add_compare_fusion.2, bf16[256,1,8,128]{3,0,2,1:T(8,128)(2,1)S(1)} %get-tuple-element.337, bf16[6144,1,256]{2,0,1:T(8,128)(2,1)} %get-tuple-element.336, s32[]{:T(128)S(6)} %select_n.218), kind=kOutput, calls=%fused_computation.3.clone.1 | convolution fusion | flops 271579136 | bytes 4858372 | tf_op jit(solution)/shard_map/while/body/eval_jaxpr/tkgd,skd->tkgs/dot_general | solution.py:64
  200.4 5.0 %fusion.59 = f32[256,1,8,128]{0,3,2,1:T(8,128)} fusion(f32[512,256,8]{1,0,2:T(8,128)} %get-tuple-element.305, f32[256,8]{0,1:T(8,128)S(1)} %bitcast.223, pred[512]{0:T(512)(128)(4,1)S(1)} %add_compare_fusion.2, f32[256,1,8,128]{0,3,2,1:T(8,128)} %get-tuple-element.322, f32[256,8]{0,1:T(8,128)S(1)} %get-tuple-element.306, pred[]{:T(512)S(6)} %compare.3, ...), kind=kOutput, calls=%fused_computation.14.clone.1 | convolution fusion | flops 274464768 | bytes 6439945 | tf_op jit(solution)/shard_map/while/body/eval_jaxpr/tkgs,skd->tkgd/dot_general | solution.py:78
  205.3 1.2 fusion.58
  206.6 3.6 %bitcast_reduce_fusion.2 = (f32[256,8]{0,1:T(8,128)S(1)}, f32[512,256,8]{1,0,2:T(8,128)}) fusion(pred[512]{0:T(512)(128)(4,1)S(1)} %add_compare_fusion.2, bf16[256,1,8,128]{3,0,2,1:T(8,128)(2,1)S(1)} %get-tuple-element.337, bf16[6144,1,256]{2,0,1:T(8,128)(2,1)} %get-tuple-element.336, s32[]{:T(128)S(6)} %select_n.218), kind=kOutput, calls=%fused_computation.3.clone.1 | convolution fusion | flops 271579136 | bytes 4858372 | tf_op jit(solution)/shard_map/while/body/eval_jaxpr/tkgd,skd->tkgs/dot_general | solution.py:64
  210.2 5.0 %fusion.59 = f32[256,1,8,128]{0,3,2,1:T(8,128)} fusion(f32[512,256,8]{1,0,2:T(8,128)} %get-tuple-element.305, f32[256,8]{0,1:T(8,128)S(1)} %bitcast.223, pred[512]{0:T(512)(128)(4,1)S(1)} %add_compare_fusion.2, f32[256,1,8,128]{0,3,2,1:T(8,128)} %get-tuple-element.322, f32[256,8]{0,1:T(8,128)S(1)} %get-tuple-element.306, pred[]{:T(512)S(6)} %compare.3, ...), kind=kOutput, calls=%fused_computation.14.clone.1 | convolution fusion | flops 274464768 | bytes 6439945 | tf_op jit(solution)/shard_map/while/body/eval_jaxpr/tkgs,skd->tkgd/dot_general | solution.py:78
  215.1 1.2 fusion.58
  216.3 3.6 %bitcast_reduce_fusion.2 = (f32[256,8]{0,1:T(8,128)S(1)}, f32[512,256,8]{1,0,2:T(8,128)}) fusion(pred[512]{0:T(512)(128)(4,1)S(1)} %add_compare_fusion.2, bf16[256,1,8,128]{3,0,2,1:T(8,128)(2,1)S(1)} %get-tuple-element.337, bf16[6144,1,256]{2,0,1:T(8,128)(2,1)} %get-tuple-element.336, s32[]{:T(128)S(6)} %select_n.218), kind=kOutput, calls=%fused_computation.3.clone.1 | convolution fusion | flops 271579136 | bytes 4858372 | tf_op jit(solution)/shard_map/while/body/eval_jaxpr/tkgd,skd->tkgs/dot_general | solution.py:64
  219.9 5.0 %fusion.59 = f32[256,1,8,128]{0,3,2,1:T(8,128)} fusion(f32[512,256,8]{1,0,2:T(8,128)} %get-tuple-element.305, f32[256,8]{0,1:T(8,128)S(1)} %bitcast.223, pred[512]{0:T(512)(128)(4,1)S(1)} %add_compare_fusion.2, f32[256,1,8,128]{0,3,2,1:T(8,128)} %get-tuple-element.322, f32[256,8]{0,1:T(8,128)S(1)} %get-tuple-element.306, pred[]{:T(512)S(6)} %compare.3, ...), kind=kOutput, calls=%fused_computation.14.clone.1 | convolution fusion | flops 274464768 | bytes 6439945 | tf_op jit(solution)/shard_map/while/body/eval_jaxpr/tkgs,skd->tkgd/dot_general | solution.py:78
  224.9 1.2 fusion.58
  226.1 3.6 %bitcast_reduce_fusion.2 = (f32[256,8]{0,1:T(8,128)S(1)}, f32[512,256,8]{1,0,2:T(8,128)}) fusion(pred[512]{0:T(512)(128)(4,1)S(1)} %add_compare_fusion.2, bf16[256,1,8,128]{3,0,2,1:T(8,128)(2,1)S(1)} %get-tuple-element.337, bf16[6144,1,256]{2,0,1:T(8,128)(2,1)} %get-tuple-element.336, s32[]{:T(128)S(6)} %select_n.218), kind=kOutput, calls=%fused_computation.3.clone.1 | convolution fusion | flops 271579136 | bytes 4858372 | tf_op jit(solution)/shard_map/while/body/eval_jaxpr/tkgd,skd->tkgs/dot_general | solution.py:64
  229.7 5.0 %fusion.59 = f32[256,1,8,128]{0,3,2,1:T(8,128)} fusion(f32[512,256,8]{1,0,2:T(8,128)} %get-tuple-element.305, f32[256,8]{0,1:T(8,128)S(1)} %bitcast.223, pred[512]{0:T(512)(128)(4,1)S(1)} %add_compare_fusion.2, f32[256,1,8,128]{0,3,2,1:T(8,128)} %get-tuple-element.322, f32[256,8]{0,1:T(8,128)S(1)} %get-tuple-element.306, pred[]{:T(512)S(6)} %compare.3, ...), kind=kOutput, calls=%fused_computation.14.clone.1 | convolution fusion | flops 274464768 | bytes 6439945 | tf_op jit(solution)/shard_map/while/body/eval_jaxpr/tkgs,skd->tkgd/dot_general | solution.py:78
  234.7 1.2 fusion.58
  235.9 3.6 %bitcast_reduce_fusion.2 = (f32[256,8]{0,1:T(8,128)S(1)}, f32[512,256,8]{1,0,2:T(8,128)}) fusion(pred[512]{0:T(512)(128)(4,1)S(1)} %add_compare_fusion.2, bf16[256,1,8,128]{3,0,2,1:T(8,128)(2,1)S(1)} %get-tuple-element.337, bf16[6144,1,256]{2,0,1:T(8,128)(2,1)} %get-tuple-element.336, s32[]{:T(128)S(6)} %select_n.218), kind=kOutput, calls=%fused_computation.3.clone.1 | convolution fusion | flops 271579136 | bytes 4858372 | tf_op jit(solution)/shard_map/while/body/eval_jaxpr/tkgd,skd->tkgs/dot_general | solution.py:64
  239.5 5.0 %fusion.59 = f32[256,1,8,128]{0,3,2,1:T(8,128)} fusion(f32[512,256,8]{1,0,2:T(8,128)} %get-tuple-element.305, f32[256,8]{0,1:T(8,128)S(1)} %bitcast.223, pred[512]{0:T(512)(128)(4,1)S(1)} %add_compare_fusion.2, f32[256,1,8,128]{0,3,2,1:T(8,128)} %get-tuple-element.322, f32[256,8]{0,1:T(8,128)S(1)} %get-tuple-element.306, pred[]{:T(512)S(6)} %compare.3, ...), kind=kOutput, calls=%fused_computation.14.clone.1 | convolution fusion | flops 274464768 | bytes 6439945 | tf_op jit(solution)/shard_map/while/body/eval_jaxpr/tkgs,skd->tkgd/dot_general | solution.py:78
  244.4 1.2 fusion.58
  245.7 3.6 %bitcast_reduce_fusion.2 = (f32[256,8]{0,1:T(8,128)S(1)}, f32[512,256,8]{1,0,2:T(8,128)}) fusion(pred[512]{0:T(512)(128)(4,1)S(1)} %add_compare_fusion.2, bf16[256,1,8,128]{3,0,2,1:T(8,128)(2,1)S(1)} %get-tuple-element.337, bf16[6144,1,256]{2,0,1:T(8,128)(2,1)} %get-tuple-element.336, s32[]{:T(128)S(6)} %select_n.218), kind=kOutput, calls=%fused_computation.3.clone.1 | convolution fusion | flops 271579136 | bytes 4858372 | tf_op jit(solution)/shard_map/while/body/eval_jaxpr/tkgd,skd->tkgs/dot_general | solution.py:64
  249.3 5.0 %fusion.59 = f32[256,1,8,128]{0,3,2,1:T(8,128)} fusion(f32[512,256,8]{1,0,2:T(8,128)} %get-tuple-element.305, f32[256,8]{0,1:T(8,128)S(1)} %bitcast.223, pred[512]{0:T(512)(128)(4,1)S(1)} %add_compare_fusion.2, f32[256,1,8,128]{0,3,2,1:T(8,128)} %get-tuple-element.322, f32[256,8]{0,1:T(8,128)S(1)} %get-tuple-element.306, pred[]{:T(512)S(6)} %compare.3, ...), kind=kOutput, calls=%fused_computation.14.clone.1 | convolution fusion | flops 274464768 | bytes 6439945 | tf_op jit(solution)/shard_map/while/body/eval_jaxpr/tkgs,skd->tkgd/dot_general | solution.py:78
  254.2 1.2 fusion.58
  255.5 3.6 %bitcast_reduce_fusion.2 = (f32[256,8]{0,1:T(8,128)S(1)}, f32[512,256,8]{1,0,2:T(8,128)}) fusion(pred[512]{0:T(512)(128)(4,1)S(1)} %add_compare_fusion.2, bf16[256,1,8,128]{3,0,2,1:T(8,128)(2,1)S(1)} %get-tuple-element.337, bf16[6144,1,256]{2,0,1:T(8,128)(2,1)} %get-tuple-element.336, s32[]{:T(128)S(6)} %select_n.218), kind=kOutput, calls=%fused_computation.3.clone.1 | convolution fusion | flops 271579136 | bytes 4858372 | tf_op jit(solution)/shard_map/while/body/eval_jaxpr/tkgd,skd->tkgs/dot_general | solution.py:64
  259.0 5.0 %fusion.59 = f32[256,1,8,128]{0,3,2,1:T(8,128)} fusion(f32[512,256,8]{1,0,2:T(8,128)} %get-tuple-element.305, f32[256,8]{0,1:T(8,128)S(1)} %bitcast.223, pred[512]{0:T(512)(128)(4,1)S(1)} %add_compare_fusion.2, f32[256,1,8,128]{0,3,2,1:T(8,128)} %get-tuple-element.322, f32[256,8]{0,1:T(8,128)S(1)} %get-tuple-element.306, pred[]{:T(512)S(6)} %compare.3, ...), kind=kOutput, calls=%fused_computation.14.clone.1 | convolution fusion | flops 274464768 | bytes 6439945 | tf_op jit(solution)/shard_map/while/body/eval_jaxpr/tkgs,skd->tkgd/dot_general | solution.py:78
  264.0 1.2 fusion.58
  265.2 3.6 %bitcast_reduce_fusion.2 = (f32[256,8]{0,1:T(8,128)S(1)}, f32[512,256,8]{1,0,2:T(8,128)}) fusion(pred[512]{0:T(512)(128)(4,1)S(1)} %add_compare_fusion.2, bf16[256,1,8,128]{3,0,2,1:T(8,128)(2,1)S(1)} %get-tuple-element.337, bf16[6144,1,256]{2,0,1:T(8,128)(2,1)} %get-tuple-element.336, s32[]{:T(128)S(6)} %select_n.218), kind=kOutput, calls=%fused_computation.3.clone.1 | convolution fusion | flops 271579136 | bytes 4858372 | tf_op jit(solution)/shard_map/while/body/eval_jaxpr/tkgd,skd->tkgs/dot_general | solution.py:64
  268.8 5.0 %fusion.59 = f32[256,1,8,128]{0,3,2,1:T(8,128)} fusion(f32[512,256,8]{1,0,2:T(8,128)} %get-tuple-element.305, f32[256,8]{0,1:T(8,128)S(1)} %bitcast.223, pred[512]{0:T(512)(128)(4,1)S(1)} %add_compare_fusion.2, f32[256,1,8,128]{0,3,2,1:T(8,128)} %get-tuple-element.322, f32[256,8]{0,1:T(8,128)S(1)} %get-tuple-element.306, pred[]{:T(512)S(6)} %compare.3, ...), kind=kOutput, calls=%fused_computation.14.clone.1 | convolution fusion | flops 274464768 | bytes 6439945 | tf_op jit(solution)/shard_map/while/body/eval_jaxpr/tkgs,skd->tkgd/dot_general | solution.py:78
  273.8 1.2 fusion.58
  275.0 2.7 copy.57
  277.7 0.5 fusion.24
  278.2 2.3 fusion.28
  280.5 0.3 copy.59
  281.1 19.1 %all_to_all.56 = bf16[8,32,1024]{2,1,0:T(8,128)(2,1)S(1)} all-to-all(bf16[8,32,1024]{2,1,0:T(8,128)(2,1)S(1)} %reshape.250), channel_id=1, replica_groups=mesh['pool'=4,'seq'=16,'tp'=8] {'tp'}, dimensions={0} | all-to-all | bytes 1048576 | tf_op jit(solution)/shard_map/all_to_all | solution.py:110
  300.2 0.8 copy.65
  (98 shorter events, 1.7 us)
Async XLA Ops:
  0.0 20.3 %copy-start = (bf16[16,128,1,256]{3,1,2,0:T(8,128)(2,1)S(1)}, bf16[16,128,1,256]{3,1,2,0:T(8,128)(2,1)}, u32[]{:S(2)}) copy-start(bf16[16,128,1,256]{3,1,2,0:T(8,128)(2,1)} %param.10) | copy-start | bytes 3145732
  1.7 14.6 %all-to-all-start.2 = ((bf16[32,8,256]{2,0,1:T(8,128)(2,1)}), bf16[32,8,256]{2,0,1:T(8,128)(2,1)S(1)}, u32[]{:S(2)}, u32[]{:S(2)}) async-start(bf16[32,8,256]{2,0,1:T(8,128)(2,1)} %bitcast.191), calls=%async_computation.2 | async-start | bytes 262144 | tf_op jit(solution)/shard_map/all_to_all | solution.py:33
  16.2 20.0 %all-to-all-start.1 = ((bf16[32,8,1024]{2,0,1:T(8,128)(2,1)}), bf16[32,8,1024]{2,0,1:T(8,128)(2,1)S(1)}, u32[]{:S(2)}, u32[]{:S(2)}) async-start(bf16[32,8,1024]{2,0,1:T(8,128)(2,1)} %copy.53), calls=%async_computation.1 | async-start | bytes 1048576 | tf_op jit(solution)/shard_map/all_to_all | solution.py:32
  27.7 24.9 %copy-start.4 = (s32[64]{0:T(128)S(1)}, s32[64]{0:T(128)}, u32[]{:S(2)}) copy-start(s32[64]{0:T(128)} %param.11) | copy-start | bytes 772
  27.7 26.1 %copy-start.3 = (s32[64,48]{0,1:T(8,128)S(1)}, s32[64,48]{0,1:T(8,128)}, u32[]{:S(2)}) copy-start(s32[64,48]{0,1:T(8,128)} %param.12) | copy-start | bytes 36868
  36.2 112.1 %all-to-all-start = ((bf16[64,1,128,1,256]{4,2,3,1,0:T(8,128)(2,1)}), bf16[64,1,128,1,256]{4,2,3,1,0:T(8,128)(2,1)}, u32[]{:S(2)}, u32[]{:S(2)}) async-start(bf16[64,1,128,1,256]{4,2,3,1,0:T(8,128)(2,1)} %bitcast_select_fusion.1), calls=%async_computation | async-start | bytes 8388608 | tf_op jit(solution)/shard_map/all_to_all | solution.py:47
  161.6 4.7 %copy-start.1 = (f32[512,256,8]{1,0,2:T(8,128)S(1)}, f32[512,256,8]{1,0,2:T(8,128)}, u32[]{:S(2)}) copy-start(f32[512,256,8]{1,0,2:T(8,128)} %get-tuple-element.305) | copy-start | bytes 12582916 | tf_op jit(solution)/shard_map/while
  171.0 5.0 %copy-start.1 = (f32[512,256,8]{1,0,2:T(8,128)S(1)}, f32[512,256,8]{1,0,2:T(8,128)}, u32[]{:S(2)}) copy-start(f32[512,256,8]{1,0,2:T(8,128)} %get-tuple-element.305) | copy-start | bytes 12582916 | tf_op jit(solution)/shard_map/while
  180.8 5.0 %copy-start.1 = (f32[512,256,8]{1,0,2:T(8,128)S(1)}, f32[512,256,8]{1,0,2:T(8,128)}, u32[]{:S(2)}) copy-start(f32[512,256,8]{1,0,2:T(8,128)} %get-tuple-element.305) | copy-start | bytes 12582916 | tf_op jit(solution)/shard_map/while
  190.6 5.0 %copy-start.1 = (f32[512,256,8]{1,0,2:T(8,128)S(1)}, f32[512,256,8]{1,0,2:T(8,128)}, u32[]{:S(2)}) copy-start(f32[512,256,8]{1,0,2:T(8,128)} %get-tuple-element.305) | copy-start | bytes 12582916 | tf_op jit(solution)/shard_map/while
  200.4 5.0 %copy-start.1 = (f32[512,256,8]{1,0,2:T(8,128)S(1)}, f32[512,256,8]{1,0,2:T(8,128)}, u32[]{:S(2)}) copy-start(f32[512,256,8]{1,0,2:T(8,128)} %get-tuple-element.305) | copy-start | bytes 12582916 | tf_op jit(solution)/shard_map/while
  210.2 5.0 %copy-start.1 = (f32[512,256,8]{1,0,2:T(8,128)S(1)}, f32[512,256,8]{1,0,2:T(8,128)}, u32[]{:S(2)}) copy-start(f32[512,256,8]{1,0,2:T(8,128)} %get-tuple-element.305) | copy-start | bytes 12582916 | tf_op jit(solution)/shard_map/while
  219.9 5.0 %copy-start.1 = (f32[512,256,8]{1,0,2:T(8,128)S(1)}, f32[512,256,8]{1,0,2:T(8,128)}, u32[]{:S(2)}) copy-start(f32[512,256,8]{1,0,2:T(8,128)} %get-tuple-element.305) | copy-start | bytes 12582916 | tf_op jit(solution)/shard_map/while
  229.7 5.0 %copy-start.1 = (f32[512,256,8]{1,0,2:T(8,128)S(1)}, f32[512,256,8]{1,0,2:T(8,128)}, u32[]{:S(2)}) copy-start(f32[512,256,8]{1,0,2:T(8,128)} %get-tuple-element.305) | copy-start | bytes 12582916 | tf_op jit(solution)/shard_map/while
  239.5 5.0 %copy-start.1 = (f32[512,256,8]{1,0,2:T(8,128)S(1)}, f32[512,256,8]{1,0,2:T(8,128)}, u32[]{:S(2)}) copy-start(f32[512,256,8]{1,0,2:T(8,128)} %get-tuple-element.305) | copy-start | bytes 12582916 | tf_op jit(solution)/shard_map/while
  249.3 5.0 %copy-start.1 = (f32[512,256,8]{1,0,2:T(8,128)S(1)}, f32[512,256,8]{1,0,2:T(8,128)}, u32[]{:S(2)}) copy-start(f32[512,256,8]{1,0,2:T(8,128)} %get-tuple-element.305) | copy-start | bytes 12582916 | tf_op jit(solution)/shard_map/while
  259.0 5.0 %copy-start.1 = (f32[512,256,8]{1,0,2:T(8,128)S(1)}, f32[512,256,8]{1,0,2:T(8,128)}, u32[]{:S(2)}) copy-start(f32[512,256,8]{1,0,2:T(8,128)} %get-tuple-element.305) | copy-start | bytes 12582916 | tf_op jit(solution)/shard_map/while
  268.8 5.0 %copy-start.1 = (f32[512,256,8]{1,0,2:T(8,128)S(1)}, f32[512,256,8]{1,0,2:T(8,128)}, u32[]{:S(2)}) copy-start(f32[512,256,8]{1,0,2:T(8,128)} %get-tuple-element.305) | copy-start | bytes 12582916 | tf_op jit(solution)/shard_map/while
  275.0 2.7 copy-start.2
where the time goes:
time: 304 us; the launch traced here: 301 us
  matrix products  106 us (35%)
  waiting for transfers between devices  102 us (34%)
  other arithmetic  27.3 us (9%)
  starting transfers between devices  27.2 us (9%)
  blocking collectives  19.1 us (6%)
  local copies, waits for them, and re-layouts  18.4 us (6%)
    all_to_all x1, waiting for transfers between devices, local(): lax.all_to_all(outgoing, ('pool', 'seq'), split_axis=0, concat_axis=0, ti...  90.4 us
    dot_general x13, matrix products, attend(): jnp.einsum('tkgs,skd->tkgd', weights.astype(jnp.bfloat16), key_block[...,...  61.4 us
    dot_general x13, matrix products, attend(): jnp.einsum('tkgd,skd->tkgs', q_heads, key_block[..., :head_dim], preferre...  44.7 us
    all_to_all x1, blocking collectives, local(): return lax.all_to_all(output, 'tp', split_axis=0, concat_axis=2, tiled=True)  19.1 us
    all_to_all x1, starting transfers between devices, local(): lax.all_to_all(outgoing, ('pool', 'seq'), split_axis=0, concat_axis=0, ti...  16.4 us
    reduce_sum x13, other arithmetic, attend(): run_total = run_total * shrink + jnp.sum(weights, axis=-1)  14.4 us
    all_to_all x1, waiting for transfers between devices, local(): lax.all_to_all(q_parts, 'tp', split_axis=1, concat_axis=0, tiled=True)  8.52 us
    all_to_all x1, starting transfers between devices, local(): lax.all_to_all(kv_parts, 'tp', split_axis=1, concat_axis=0, tiled=True)  6.82 us
  transfers between devices with their start and end apart: 3, of which 3 were waited for; matrix products, arithmetic and copies ran while one was open for 6% of the time, Pallas kernels for 0%

commit v1 on v0

v1 whole, which is shorter than its diff:
```python
import functools
import math

import jax
import jax.numpy as jnp
from jax import lax
from jax.experimental import pallas as pl
from jax.experimental.pallas import tpu as pltpu
from jax.sharding import Mesh
from jax.sharding import PartitionSpec as P

QH = 64
KVH = 8
GROUP = QH // KVH
MASKED_SCORE = -1e30
PLANE = ("pool", "core")


def pick_kernel(plans, place, table, *refs):
    buffers, (out, sem) = refs[:-2], refs[-2:]
    x, z, c = place[0], place[1], place[2]
    pools, planes, cores = place[3], place[4], place[5]
    way = 1 - 2 * c
    copies = []
    for buffer, request_step, owner_step, column in plans:
        for peer in range(out.shape[0]):
            if request_step is None:
                slot = peer
            else:
                request_z = lax.rem(z + request_step * way + planes, planes)
                owner_z = lax.rem(z + owner_step * way + planes, planes)
                request = (peer // 2 * planes + request_z) * cores + peer % 2
                owner = (x * planes + owner_z) * cores + c
                slot = jnp.maximum(table[request, owner] - 1, 0)
            copy = pltpu.make_async_copy(buffers[buffer].at[slot], out.at[peer, column], sem)
            copy.start()
            copies.append(copy)
    for copy in copies:
        copy.wait()


def pick(place, table, buffers, plans, peers):
    block = buffers[0].shape[1:]
    columns = len(plans)
    return pl.pallas_call(
        functools.partial(pick_kernel, plans),
        grid_spec=pltpu.PrefetchScalarGridSpec(
            num_scalar_prefetch=2,
            grid=(1,),
            in_specs=[pl.BlockSpec(memory_space=pl.ANY)] * len(buffers),
            out_specs=pl.BlockSpec((peers, columns) + block, lambda *_: (0, 0, 0, 0)),
            scratch_shapes=[pltpu.SemaphoreType.DMA],
        ),
        out_shape=jax.ShapeDtypeStruct((peers, columns) + block, buffers[0].dtype),
    )(place, table, *buffers)


def attend_kernel(rounds, chunk, first, last, scale, place, table, *refs):
    refs = list(refs)
    q_ref = refs.pop(0)
    arrived = [refs.pop(0) for _ in rounds]
    if not first:
        acc_in, ml_in = refs.pop(0), refs.pop(0)
    if last:
        out_ref = refs.pop(0)
    else:
        acc_out, ml_out = refs.pop(0), refs.pop(0)
    turned = refs.pop(0) if first else q_ref
    blocks, acc, ml, sem = refs
    if not last:
        acc, ml = acc_out, ml_out
    x, z, c = place[0], place[1], place[2]
    planes, cores = place[4], place[5]
    me = (x * planes + z) * cores + c
    group, head_dim, tokens = acc.shape
    block_len = arrived[0].shape[2]

    def fetch(source, at):
        return pltpu.make_async_copy(source, blocks.at[pl.ds(at * block_len, block_len)], sem)

    count = jnp.int32(0)
    for array, steps in zip(arrived, rounds):
        for lane in range(array.shape[0]):
            way = 1 - 2 * (lane % 2)
            for column in range(array.shape[1]):
                owner_z = lax.rem(z + steps[column] * way + planes, planes)
                live = table[me, (lane // 2 * planes + owner_z) * cores + lane % 2] > 0

                @pl.when(live)
                def _():
                    fetch(array.at[lane, column], count).start()

                count = count + live.astype(jnp.int32)
    chunks = (count + chunk - 1) // chunk
    spare = arrived[0].at[0, 0]

    def fill(at, carried):
        fetch(spare, at).start()
        return carried

    def drain(at, carried):
        fetch(spare, at).wait()
        return carried

    lax.fori_loop(count, chunks * chunk, fill, 0)

    def scores_of(head, keys):
        query = turned[head * head_dim : (head + 1) * head_dim, :]
        return jnp.dot(keys, query, preferred_element_type=jnp.float32)

    def absorb(pending):
        head, weights, values, shrink = pending
        add = jnp.dot(values, weights, preferred_element_type=jnp.float32)
        acc[head] = add if shrink is None else acc[head] * shrink + add

    def sweep(keys, values, mask, fresh):
        score, pending = scores_of(0, keys), None
        for head in range(group):
            ahead = scores_of(head + 1, keys) if head + 1 < group else None
            score = mask(score)
            top = jnp.max(score, axis=0, keepdims=True)
            shrink = None
            if not fresh:
                old = ml[0, head : head + 1, :]
                top = jnp.maximum(top, old)
                shrink = jnp.exp2((old - top) * scale)
            weights = jnp.exp2((score - top) * scale)
            total = jnp.sum(weights, axis=0, keepdims=True)
            ml[1, head : head + 1, :] = total if fresh else ml[1, head : head + 1, :] * shrink + total
            ml[0, head : head + 1, :] = top
            if pending is not None:
                absorb(pending)
            pending = (head, weights.astype(values.dtype), values, shrink)
            score = ahead
        absorb(pending)

    if first:
        turned[...] = q_ref[:, : group * head_dim].T
        own = q_ref[:, group * head_dim :]
        key = lax.broadcasted_iota(jnp.int32, (tokens, tokens), 0)
        token = lax.broadcasted_iota(jnp.int32, (tokens, tokens), 1)
        sweep(own[:, :head_dim], own[:, head_dim:].T, lambda s: jnp.where(key <= token, s, MASKED_SCORE), True)
    else:
        acc[...] = acc_in[...]
        ml[...] = ml_in[...]
    lax.fori_loop(0, chunks * chunk, drain, 0)

    def body(at, carried):
        size = chunk * block_len
        kv = blocks[pl.ds(pl.multiple_of(at * size, size), size), :]

        def mask(score):
            parts = [score[:block_len]]
            for b in range(1, chunk):
                part = score[b * block_len : (b + 1) * block_len]
                parts.append(jnp.where(at * chunk + b < count, part, MASKED_SCORE))
            return jnp.concatenate(parts, axis=0)

        sweep(kv[:, :head_dim], kv[:, head_dim:].T, mask, False)
        return carried

    lax.fori_loop(0, chunks, body, 0)
    if last:
        for head in range(group):
            done = acc[head] / ml[1, head : head + 1, :]
            out_ref[:, head * head_dim : (head + 1) * head_dim] = done.T.astype(out_ref.dtype)


def attend(place, table, query, arrived, rounds, state, last, scale, group, head_dim, tokens, chunk=8):
    first = state is None
    dtype = arrived[0].dtype
    slots = sum(array.shape[0] * array.shape[1] for array in arrived)
    slots = (slots + chunk - 1) // chunk * chunk
    block_len = arrived[0].shape[2]
    whole = pl.BlockSpec(memory_space=pltpu.VMEM)
    operands = [query] + list(arrived) + ([] if first else list(state))
    in_specs = [whole] + [pl.BlockSpec(memory_space=pl.ANY)] * len(arrived) + ([] if first else [whole] * 2)
    acc = ((group, head_dim, tokens), jnp.float32)
    ml = ((2, group, tokens), jnp.float32)
    outs = [((tokens, group * head_dim), dtype)] if last else [acc, ml]
    if first:
        outs.append(((group * head_dim, tokens), dtype))
    return pl.pallas_call(
        functools.partial(attend_kernel, rounds, chunk, first, last, scale * math.log2(math.e)),
        grid_spec=pltpu.PrefetchScalarGridSpec(
            num_scalar_prefetch=2,
            grid=(1,),
            in_specs=in_specs,
            out_specs=[whole] * len(outs),
            scratch_shapes=[
                pltpu.VMEM((slots * block_len, 2 * head_dim), dtype),
                pltpu.VMEM(*acc),
                pltpu.VMEM(*ml),
                pltpu.SemaphoreType.DMA,
            ],
        ),
        out_shape=[jax.ShapeDtypeStruct(*out) for out in outs],
        compiler_params=pltpu.CompilerParams(vmem_limit_bytes=48 * 1024 * 1024),
    )(place, table, query, *operands[1:])


def local(queries, stretch_kv, pool_kv, prefix_blocks, block_owner, block_slot):
    pools, planes, cores = lax.axis_size("pool"), lax.axis_size("z"), lax.axis_size("core")
    x, z, c = lax.axis_index("pool"), lax.axis_index("z"), lax.axis_index("core")
    tensor_count = lax.axis_size("tp")
    owner_count = pools * planes * cores
    peers = pools * cores
    tok_local = queries.shape[1]
    block_len, pair = pool_kv.shape[1], pool_kv.shape[3]
    head_dim = pair // 2
    scale = 1.0 / math.sqrt(head_dim)
    max_blocks = block_owner.shape[1]
    pool = pool_kv.reshape(-1, block_len, pair)

    def hop(array, long):
        pairs = []
        for at in range(planes):
            for core in range(cores):
                way = (1 if core == 0 else -1) * (1 if long else -1)
                pairs.append((at * cores + core, (at + way) % planes * cores + core))
        return lax.ppermute(array, ("z", "core"), pairs)

    def deliver(array):
        return lax.all_to_all(array, PLANE, split_axis=0, concat_axis=0, tiled=True)

    long1, short1 = hop(pool, True), hop(pool, False)

    place = jnp.stack([x, z, c, jnp.int32(pools), jnp.int32(planes), jnp.int32(cores)]).astype(jnp.int32)
    position = jnp.arange(max_blocks, dtype=jnp.int32)
    live = position[None, :] < prefix_blocks[:, None]
    owners = jnp.arange(owner_count, dtype=jnp.int32)
    table = jnp.sum(
        jnp.where(
            (block_owner[:, :, None] == owners[None, None, :]) & live[:, :, None],
            block_slot[:, :, None] + 1,
            0,
        ),
        axis=1,
    )

    both = jnp.concatenate([queries[0].reshape(tok_local, tensor_count, -1), stretch_kv[0]], axis=2)
    q_kv = lax.all_to_all(both, "tp", split_axis=1, concat_axis=0, tiled=True)
    q_kv = q_kv.reshape(tok_local * tensor_count, -1)

    tokens = q_kv.shape[0]
    get = functools.partial(pick, place, table, peers=peers)
    step = functools.partial(
        attend, place, table, scale=scale, group=GROUP, head_dim=head_dim, tokens=tokens
    )
    half = planes // 2
    longs, shorts = [pool, long1], [pool, short1]
    waiting, rounds = [deliver(get([pool], ((0, 0, 0, 0),)))], [(0,)]
    query, state = q_kv, None
    for k in range(1, half):
        if k + 1 < half:
            longs.append(hop(longs[k], True))
        else:
            longs.append(hop(get([longs[k]], ((0, 1, -k, 0),)), True))
        if k + 1 < half - 1:
            shorts.append(hop(shorts[k], False))
        elif k + 1 == half - 1:
            shorts.append(hop(get([shorts[k]], ((0, -1, k, 0),)), False))
        source, short = longs[k], shorts[k]
        if k > 1:
            made = step(query, waiting, tuple(rounds), state, False)
            if state is None:
                query = made[2]
            state = made[:2]
            waiting, rounds = [arriving], [arriving_round]
            source, short, *state = lax.optimization_barrier((source, short, *state))
        if k < half - 1:
            out = get([source, short], ((0, 0, -k, 0), (1, 0, k, 1)))
        else:
            short = short.reshape((peers,) + short.shape[2:])
            out = get([source, short], ((0, 0, -k, 0), (1, None, None, 1)))
        arriving, arriving_round = deliver(out), (-k, k)
    waiting, rounds = waiting + [arriving], rounds + [arriving_round]
    final = deliver(longs[half])
    *state, = step(query, waiting, tuple(rounds), state, False)
    (attended,) = step(query, [final], ((-half,),), state, True)
    attended = attended.reshape(tensor_count, tok_local, -1)
    attended = lax.all_to_all(attended, "tp", split_axis=0, concat_axis=2, tiled=True)
    return attended


def solution(mesh):
    pools, seq, tensor = mesh.devices.shape
    fine = Mesh(mesh.devices.reshape(pools, seq // 2, 2, tensor), ("pool", "z", "core", "tp"))
    rows = ("pool", "z", "core")
    return jax.shard_map(
        local,
        mesh=fine,
        in_specs=(
            P(rows, "tp", None),
            P(rows, "tp", None, None),
            P(rows, None, "tp", None),
            P(),
            P(),
            P(),
        ),
        out_specs=P(rows, "tp", None),
        check_vma=False,
    )
```

time: 304 us -> 191 us (0.63)
  matrix products: 106 us -> 0 us
  waiting for transfers between devices: 102 us -> 33.1 us
  Pallas kernels: 0 us -> 49.3 us
  starting transfers between devices: 27.2 us -> 65.5 us
  other arithmetic: 27.3 us -> 4.7 us
  local copies, waits for them, and re-layouts: 18.4 us -> 11.2 us
  blocking collectives: 19.1 us -> 23.1 us
    dot_general x26 -> x0, matrix products: 106 us -> none  [the longest x13 61.4 us: attend(): jnp.einsum('tkgs,skd->tkgd', weights.astype(jnp.bfloat16), key_block[...,...]
    all_to_all x3 -> x6, waiting for transfers between devices: 102 us -> 0.02 us  [the longest x5 0.01 us: deliver(): return lax.all_to_all(array, PLANE, split_axis=0, concat_axis=0, tiled=True)]
    pallas_call x0 -> x10, Pallas kernels: none -> 49.3 us  [the longest x4 29 us: attend(): pl.pallas_call(functools.partial(attend_kernel, rounds, chunk, first, las...]
    ppermute x0 -> x7, waiting for transfers between devices: none -> 33 us  [hop(): return lax.ppermute(array, ('z', 'core'), pairs)]
    ppermute x0 -> x7, starting transfers between devices: none -> 26.4 us  [hop(): return lax.ppermute(array, ('z', 'core'), pairs)]
    reduce_sum x15 -> x1, other arithmetic: 14.7 us -> 2.33 us  [local(): jnp.sum(jnp.where((block_owner[:, :, None] == owners[None, None, :]) & li...]
    all_to_all x3 -> x6, starting transfers between devices: 27.2 us -> 39.1 us  [the longest x5 32.3 us: deliver(): return lax.all_to_all(array, PLANE, split_axis=0, concat_axis=0, tiled=True)]
    select_n x4 -> x0, other arithmetic: 10.1 us -> none  [the longest x2 5.49 us: local(): jnp.take(arrived, source, axis=0)]
  transfers between devices with their start and end apart: 3 -> 13, of which waited for: 3 -> 4; matrix products, arithmetic and copies ran while one was open for 6% -> 1% of each run, Pallas kernels for 0% -> 22%
where the time goes in v1:
time: 191 us; the launch traced here: 187 us
  starting transfers between devices  65.5 us (34%)
  Pallas kernels  49.3 us (26%)
  waiting for transfers between devices  33.1 us (17%)
  blocking collectives  23.1 us (12%)
  local copies, waits for them, and re-layouts  11.2 us (6%)
  other arithmetic  4.7 us (2%)
    ppermute x7, waiting for transfers between devices, hop(): return lax.ppermute(array, ('z', 'core'), pairs)  33 us
    all_to_all x5, starting transfers between devices, deliver(): return lax.all_to_all(array, PLANE, split_axis=0, concat_axis=0, tiled=True)  32.3 us
    pallas_call x4, Pallas kernels, attend(): pl.pallas_call(functools.partial(attend_kernel, rounds, chunk, first, las...  29 us
    ppermute x7, starting transfers between devices, hop(): return lax.ppermute(array, ('z', 'core'), pairs)  26.4 us
    all_to_all x1, blocking collectives, local(): lax.all_to_all(attended, 'tp', split_axis=0, concat_axis=2, tiled=True)  23.1 us
    pallas_call x6, Pallas kernels, pick(): pl.pallas_call(functools.partial(pick_kernel, plans), grid_spec=pltpu.Pre...  20.3 us
    unnamed x36, local copies, waits for them, and re-layouts  9.3 us
    all_to_all x1, starting transfers between devices, local(): q_kv = lax.all_to_all(both, 'tp', split_axis=1, concat_axis=0, tiled=True)  6.82 us
  transfers between devices with their start and end apart: 13, of which 4 were waited for; matrix products, arithmetic and copies ran while one was open for 1% of the time, Pallas kernels for 22%

profile of v1, /device:TPU:7, one launch (start us, length us, event | category | flops | bytes accessed | tf_op | source)
XLA Modules:
  0.0 187.2 jit_solution(14404234561804449209)
XLA Ops:
  0.0 0.7 iota_compare_fusion.1
  0.7 0.7 broadcast_add_fusion
  1.5 0.1 copy.14
  1.6 0.8 copy.13
  2.4 2.3 %select_reduce_fusion.table = s32[64,64]{1,0:T(8,128)} fusion(s32[64,48]{1,0:T(8,128)S(1)} %copy.14, s32[64,48]{1,0:T(8,128)S(1)} %copy.13, pred[64,48]{1,0:T(8,128)(4,1)S(1)} %iota_compare_fusion.1), kind=kLoop, calls=%fused_computation | loop fusion | flops 782336 | bytes 44032 | tf_op jit(solution)/shard_map/reduce_sum | solution.py:232
  4.7 0.7 stack.15.place
  5.4 3.3 %shard_map.64 = bf16[8,1,128,256]{3,2,1,0:T(8,128)(2,1)} custom-call(s32[6]{0:T(128)} %stack.15.place, s32[64,64]{1,0:T(8,128)} %select_reduce_fusion.table, bf16[16,128,256]{2,1,0:T(8,128)(2,1)} %bitcast.25), custom_call_target="tpu_custom_call" | custom-call | tf_op jit(solution)/shard_map/pallas_call | solution.py:45
  8.6 0.0 copy-start.13
  8.7 9.7 %all-to-all-start.1 = ((bf16[8,1,128,256]{3,2,1,0:T(8,128)(2,1)}), bf16[8,1,128,256]{3,2,1,0:T(8,128)(2,1)S(1)}, u32[]{:S(2)}, u32[]{:S(2)}) async-start(bf16[8,1,128,256]{3,2,1,0:T(8,128)(2,1)} %shard_map.64), calls=%async_computation.1 | async-start | bytes 1048576 | tf_op jit(solution)/shard_map/all_to_all | solution.py:224
  18.4 0.0 copy-done.12
  18.4 1.9 %collective-permute-start.4 = (bf16[16,128,256]{2,1,0:T(8,128)(2,1)S(1)}, bf16[16,128,256]{2,1,0:T(8,128)(2,1)}, u32[]{:S(2)}, u32[]{:S(2)}) collective-permute-start(bf16[16,128,256]{2,1,0:T(8,128)(2,1)S(1)} %bitcast.26), channel_id=1, source_target_pairs={{0,112},{8,24},{16,0},{24,40},{32,16},{40,56},{48,32},{56,72},{64,... | collective-permute-start | bytes 3145736 | tf_op jit(solution)/shard_map/ppermute | solution.py:221
  20.3 6.2 %collective-permute-start = (bf16[16,128,256]{2,1,0:T(8,128)(2,1)S(1)}, bf16[16,128,256]{2,1,0:T(8,128)(2,1)}, u32[]{:S(2)}, u32[]{:S(2)}) collective-permute-start(bf16[16,128,256]{2,1,0:T(8,128)(2,1)S(1)} %bitcast.27), channel_id=1, source_target_pairs={{0,16},{8,120},{16,32},{24,8},{32,48},{40,24},{48,64},{56,40},{64,... | collective-permute-start | bytes 3145736 | tf_op jit(solution)/shard_map/ppermute | solution.py:221
  26.4 0.0 copy-done.16
  26.5 0.0 copy-done.13
  26.5 0.3 copy.20
  26.8 0.3 copy.15
  27.1 0.9 pad_maximum_fusion
  28.0 0.0 all-to-all-done.1.refs_1_
  28.0 6.8 %all-to-all-start = ((bf16[32,8,1280]{2,0,1:T(8,128)(2,1)}), bf16[32,8,1280]{2,0,1:T(8,128)(2,1)S(1)}, u32[]{:S(2)}, u32[]{:S(2)}) async-start(bf16[32,8,1280]{2,0,1:T(8,128)(2,1)} %pad_maximum_fusion), calls=%async_computation | async-start | bytes 1310720 | tf_op jit(solution)/shard_map/all_to_all | solution.py:242
  34.8 13.5 %collective-permute-done.refs_0_ = bf16[16,128,256]{2,1,0:T(8,128)(2,1)} collective-permute-done((bf16[16,128,256]{2,1,0:T(8,128)(2,1)S(1)}, bf16[16,128,256]{2,1,0:T(8,128)(2,1)}, u32[]{:S(2)}, u32[]{:S(2)}) %collective-permute-start) | collective-permute-done | bytes 1048608 | tf_op jit(solution)/shard_map/ppermute | solution.py:221
  48.3 5.3 %collective-permute-start.1 = (bf16[16,128,256]{2,1,0:T(8,128)(2,1)}, bf16[16,128,256]{2,1,0:T(8,128)(2,1)}, u32[]{:S(2)}, u32[]{:S(2)}) collective-permute-start(bf16[16,128,256]{2,1,0:T(8,128)(2,1)} %collective-permute-done.refs_0_), channel_id=1, source_target_pairs={{0,16},{8,120},{16,32},{24,8},{32,48},{40,24},{48,64},{56,40},{64,... | collective-permute-start | bytes 3145736 | tf_op jit(solution)/shard_map/ppermute | solution.py:221
  53.6 0.0 collective-permute-done.4.refs_1_
  53.6 1.9 %collective-permute-start.5 = (bf16[16,128,256]{2,1,0:T(8,128)(2,1)}, bf16[16,128,256]{2,1,0:T(8,128)(2,1)}, u32[]{:S(2)}, u32[]{:S(2)}) collective-permute-start(bf16[16,128,256]{2,1,0:T(8,128)(2,1)} %collective-permute-done.4.refs_1_), channel_id=1, source_target_pairs={{0,112},{8,24},{16,0},{24,40},{32,16},{40,56},{48,32},{56,72},{64,... | collective-permute-start | bytes 3145736 | tf_op jit(solution)/shard_map/ppermute | solution.py:221
  55.5 3.5 %shard_map.69 = bf16[8,2,128,256]{3,2,1,0:T(8,128)(2,1)} custom-call(s32[6]{0:T(128)} %stack.15.place, s32[64,64]{1,0:T(8,128)} %select_reduce_fusion.table, bf16[16,128,256]{2,1,0:T(8,128)(2,1)} %collective-permute-done.refs_0_, bf16[16,128,256]{2,1,0:T(8,128)(2,1)} %collective-permute-done.4.refs_1_), custom_call_target="tpu_custom_call" | custom-call | tf_op jit(solution)/shard_map/pallas_call | solution.py:45
  59.1 0.0 all-to-all-done
  59.1 4.7 %all-to-all-start.4 = ((bf16[8,2,128,256]{3,2,1,0:T(8,128)(2,1)}), bf16[8,2,128,256]{3,2,1,0:T(8,128)(2,1)S(1)}, u32[]{:S(2)}, u32[]{:S(2)}) async-start(bf16[8,2,128,256]{3,2,1,0:T(8,128)(2,1)} %shard_map.69), calls=%async_computation.4 | async-start | bytes 2097152 | tf_op jit(solution)/shard_map/all_to_all | solution.py:224
  63.8 10.7 %collective-permute-done.1.refs_0_ = bf16[16,128,256]{2,1,0:T(8,128)(2,1)} collective-permute-done((bf16[16,128,256]{2,1,0:T(8,128)(2,1)}, bf16[16,128,256]{2,1,0:T(8,128)(2,1)}, u32[]{:S(2)}, u32[]{:S(2)}) %collective-permute-start.1) | collective-permute-done | bytes 1048608 | tf_op jit(solution)/shard_map/ppermute | solution.py:221
  74.5 5.3 %collective-permute-start.2 = (bf16[16,128,256]{2,1,0:T(8,128)(2,1)}, bf16[16,128,256]{2,1,0:T(8,128)(2,1)}, u32[]{:S(2)}, u32[]{:S(2)}) collective-permute-start(bf16[16,128,256]{2,1,0:T(8,128)(2,1)} %collective-permute-done.1.refs_0_), channel_id=1, source_target_pairs={{0,16},{8,120},{16,32},{24,8},{32,48},{40,24},{48,64},{56,40},{64,... | collective-permute-start | bytes 3145736 | tf_op jit(solution)/shard_map/ppermute | solution.py:221
  79.8 0.0 copy-done
  79.8 0.0 copy-done.9
  79.8 6.0 %shard_map.65 = (f32[8,128,256]{2,1,0:T(8,128)S(1)}, f32[2,8,256]{2,1,0:T(8,128)S(1)}, bf16[1024,256]{1,0:T(8,128)(2,1)S(1)}) custom-call(s32[6]{0:T(128)S(1)} %copy-done.9, s32[64,64]{1,0:T(8,128)S(1)} %copy-done, bf16[256,1280]{1,0:T(8,128)(2,1)S(1)} %bitcast.21, bf16[8,1,128,256]{3,2,1,0:T(8,128)(2,1)S(1)} %all-to-all-done.1.refs_1_), custom_call_target="tpu_custom_call" | custom-call | tf_op jit(solution)/shard_map/pallas_call | solution.py:183
  85.8 0.0 copy-start.3
  85.9 0.9 copy-done.3
  86.8 0.0 collective-permute-done.5.refs_1_.refs_0_
  86.8 3.6 %shard_map.67 = bf16[8,2,128,256]{3,2,1,0:T(8,128)(2,1)} custom-call(s32[6]{0:T(128)} %stack.15.place, s32[64,64]{1,0:T(8,128)} %select_reduce_fusion.table, bf16[16,128,256]{2,1,0:T(8,128)(2,1)} %collective-permute-done.1.refs_0_, bf16[16,128,256]{2,1,0:T(8,128)(2,1)} %collective-permute-done.5.refs_1_.refs_0_), custom_call_target="tpu_custom_call" | custom-call | tf_op jit(solution)/shard_map/pallas_call | solution.py:45
  90.4 0.0 all-to-all-done.4.refs_1_
  90.4 4.6 %all-to-all-start.3 = ((bf16[8,2,128,256]{3,2,1,0:T(8,128)(2,1)}), bf16[8,2,128,256]{3,2,1,0:T(8,128)(2,1)S(1)}, u32[]{:S(2)}, u32[]{:S(2)}) async-start(bf16[8,2,128,256]{3,2,1,0:T(8,128)(2,1)} %shard_map.67), calls=%async_computation.3 | async-start | bytes 2097152 | tf_op jit(solution)/shard_map/all_to_all | solution.py:224
  95.0 3.3 %shard_map.68 = bf16[8,1,128,256]{3,2,1,0:T(8,128)(2,1)} custom-call(s32[6]{0:T(128)} %stack.15.place, s32[64,64]{1,0:T(8,128)} %select_reduce_fusion.table, bf16[16,128,256]{2,1,0:T(8,128)(2,1)} %collective-permute-done.5.refs_1_.refs_0_), custom_call_target="tpu_custom_call" | custom-call | tf_op jit(solution)/shard_map/pallas_call | solution.py:45
  98.3 1.9 %collective-permute-start.6 = (bf16[8,1,128,256]{3,2,0,1:T(8,128)(2,1)}, bf16[8,1,128,256]{3,2,0,1:T(8,128)(2,1)S(1)}, u32[]{:S(2)}, u32[]{:S(2)}) collective-permute-start(bf16[8,1,128,256]{3,2,0,1:T(8,128)(2,1)} %bitcast.29), channel_id=1, source_target_pairs={{0,112},{8,24},{16,0},{24,40},{32,16},{40,56},{48,32},{56,72},{64,... | collective-permute-start | bytes 1572872 | tf_op jit(solution)/shard_map/ppermute | solution.py:221
  100.3 1.2 copy-done.4
  101.5 5.0 %shard_map.70 = (f32[8,128,256]{2,1,0:T(8,128)S(1)}, f32[2,8,256]{2,1,0:T(8,128)S(1)}) custom-call(s32[6]{0:T(128)S(1)} %copy-done.10, s32[64,64]{1,0:T(8,128)S(1)} %copy-done.1, bf16[1024,256]{1,0:T(8,128)(2,1)S(1)} %get-tuple-element.20.refs_0_, bf16[8,2,128,256]{3,2,1,0:T(8,128)(2,1)S(1)} %all-to-all-done.4.refs_1_, f32[8,128,256]{2,1,0:T(8,128)S(1)} %copy-done.4, ...), custom_call_target="tpu_custom_call" | custom-call | tf_op jit(solution)/shard_map/pallas_call | solution.py:183
  106.5 1.0 copy-done.7
  107.5 2.1 %collective-permute-done.6 = bf16[8,1,128,256]{3,2,0,1:T(8,128)(2,1)S(1)} collective-permute-done((bf16[8,1,128,256]{3,2,0,1:T(8,128)(2,1)}, bf16[8,1,128,256]{3,2,0,1:T(8,128)(2,1)S(1)}, u32[]{:S(2)}, u32[]{:S(2)}) %collective-permute-start.6) | collective-permute-done | bytes 524320 | tf_op jit(solution)/shard_map/ppermute | solution.py:221
  109.7 0.0 collective-permute-done.2.refs_0_
  109.7 0.8 copy-done.15
  110.5 3.4 %shard_map.71 = bf16[8,2,128,256]{3,2,1,0:T(8,128)(2,1)} custom-call(s32[6]{0:T(128)} %stack.15.place, s32[64,64]{1,0:T(8,128)} %select_reduce_fusion.table, bf16[16,128,256]{2,1,0:T(8,128)(2,1)} %collective-permute-done.2.refs_0_, bf16[8,128,256]{2,1,0:T(8,128)(2,1)} %bitcast.30), custom_call_target="tpu_custom_call" | custom-call | tf_op jit(solution)/shard_map/pallas_call | solution.py:45
  113.9 0.0 all-to-all-done.3.refs_1_
  113.9 6.6 %all-to-all-start.5 = ((bf16[8,2,128,256]{3,2,1,0:T(8,128)(2,1)}), bf16[8,2,128,256]{3,2,1,0:T(8,128)(2,1)S(1)}, u32[]{:S(2)}, u32[]{:S(2)}) async-start(bf16[8,2,128,256]{3,2,1,0:T(8,128)(2,1)} %shard_map.71), calls=%async_computation.5 | async-start | bytes 2097152 | tf_op jit(solution)/shard_map/all_to_all | solution.py:224
  120.5 3.2 %shard_map.66 = bf16[8,1,128,256]{3,2,1,0:T(8,128)(2,1)} custom-call(s32[6]{0:T(128)} %stack.15.place, s32[64,64]{1,0:T(8,128)} %select_reduce_fusion.table, bf16[16,128,256]{2,1,0:T(8,128)(2,1)} %collective-permute-done.2.refs_0_), custom_call_target="tpu_custom_call" | custom-call | tf_op jit(solution)/shard_map/pallas_call | solution.py:45
  123.7 3.8 %collective-permute-start.3 = (bf16[8,1,128,256]{3,2,1,0:T(8,128)(2,1)}, bf16[8,1,128,256]{3,2,1,0:T(8,128)(2,1)S(1)}, u32[]{:S(2)}, u32[]{:S(2)}) collective-permute-start(bf16[8,1,128,256]{3,2,1,0:T(8,128)(2,1)} %shard_map.66), channel_id=1, source_target_pairs={{0,16},{8,120},{16,32},{24,8},{32,48},{40,24},{48,64},{56,40},{64,... | collective-permute-start | bytes 1572872 | tf_op jit(solution)/shard_map/ppermute | solution.py:221
  127.5 6.7 %collective-permute-done.3 = bf16[8,1,128,256]{3,2,1,0:T(8,128)(2,1)S(1)} collective-permute-done((bf16[8,1,128,256]{3,2,1,0:T(8,128)(2,1)}, bf16[8,1,128,256]{3,2,1,0:T(8,128)(2,1)S(1)}, u32[]{:S(2)}, u32[]{:S(2)}) %collective-permute-start.3) | collective-permute-done | bytes 524320 | tf_op jit(solution)/shard_map/ppermute | solution.py:221
  134.3 0.8 copy-done.14
  135.1 0.0 all-to-all-done.5.refs_2_
  135.1 6.8 %all-to-all-start.2 = ((bf16[8,1,128,256]{3,2,1,0:T(8,128)(2,1)}), bf16[8,1,128,256]{3,2,1,0:T(8,128)(2,1)S(1)}, u32[]{:S(2)}, u32[]{:S(2)}) async-start(bf16[8,1,128,256]{3,2,1,0:T(8,128)(2,1)} %copy-done.14), calls=%async_computation.2 | async-start | bytes 1048576 | tf_op jit(solution)/shard_map/all_to_all | solution.py:224
  141.9 0.0 copy-done.2
  141.9 1.2 copy-done.8
  143.1 12.8 %shard_map.72 = (f32[8,128,256]{2,1,0:T(8,128)S(1)}, f32[2,8,256]{2,1,0:T(8,128)S(1)}) custom-call(s32[6]{0:T(128)S(1)} %copy-done.11, s32[64,64]{1,0:T(8,128)S(1)} %copy-done.2, bf16[1024,256]{1,0:T(8,128)(2,1)S(1)} %get-tuple-element.20.refs_0_, bf16[8,2,128,256]{3,2,1,0:T(8,128)(2,1)S(1)} %all-to-all-done.3.refs_1_, ...), custom_call_target="tpu_custom_call" | custom-call | tf_op jit(solution)/shard_map/pallas_call | solution.py:183
  155.9 0.0 copy-start.5
  155.9 1.0 copy-done.5
  156.9 0.0 all-to-all-done.2.refs_1_
  156.9 1.2 copy-done.6
  158.1 5.2 %shard_map.73 = bf16[256,1024]{1,0:T(8,128)(2,1)S(1)} custom-call(s32[6]{0:T(128)S(1)} %copy-done.11, s32[64,64]{1,0:T(8,128)S(1)} %copy-done.2, bf16[1024,256]{1,0:T(8,128)(2,1)S(1)} %get-tuple-element.20.refs_0_, bf16[8,1,128,256]{3,2,1,0:T(8,128)(2,1)S(1)} %all-to-all-done.2.refs_1_, f32[8,128,256]{2,1,0:T(8,128)S(1)} %copy-done.6, ...), custom_call_target="tpu_custom_call" | custom-call | tf_op jit(solution)/shard_map/pallas_call | solution.py:183
  163.3 23.1 %all_to_all.58 = bf16[8,32,1024]{2,1,0:T(8,128)(2,1)S(1)} all-to-all(bf16[8,32,1024]{2,1,0:T(8,128)(2,1)S(1)} %bitcast.22), channel_id=1, replica_groups=mesh['pool'=4,'z'=8,'core'=2,'tp'=8] {'tp'}, dimensions={0} | all-to-all | bytes 1048576 | tf_op jit(solution)/shard_map/all_to_all | solution.py:282
  186.4 0.8 copy.19
  (18 shorter events, 0.1 us)
Async XLA Ops:
  5.4 13.0 %copy-start.12 = (bf16[16,128,1,256]{3,1,2,0:T(8,128)(2,1)S(1)}, bf16[16,128,1,256]{3,1,2,0:T(8,128)(2,1)}, u32[]{:S(2)}) copy-start(bf16[16,128,1,256]{3,1,2,0:T(8,128)(2,1)} %param.8) | copy-start | bytes 3145732
  5.4 21.1 %copy-start.16 = (bf16[1,32,8,256]{3,2,1,0:T(8,128)(2,1)S(1)}, bf16[1,32,8,256]{3,2,1,0:T(8,128)(2,1)}, u32[]{:S(2)}) copy-start(bf16[1,32,8,256]{3,2,1,0:T(8,128)(2,1)} %param.7) | copy-start | bytes 393220
  8.6 17.9 %copy-start.13 = (bf16[1,32,8192]{2,1,0:T(8,128)(2,1)S(1)}, bf16[1,32,8192]{2,1,0:T(8,128)(2,1)}, u32[]{:S(2)}) copy-start(bf16[1,32,8192]{2,1,0:T(8,128)(2,1)} %param.6) | copy-start | bytes 1572868
  8.7 19.4 %all-to-all-start.1 = ((bf16[8,1,128,256]{3,2,1,0:T(8,128)(2,1)}), bf16[8,1,128,256]{3,2,1,0:T(8,128)(2,1)S(1)}, u32[]{:S(2)}, u32[]{:S(2)}) async-start(bf16[8,1,128,256]{3,2,1,0:T(8,128)(2,1)} %shard_map.64), calls=%async_computation.1 | async-start | bytes 1048576 | tf_op jit(solution)/shard_map/all_to_all | solution.py:224
  18.4 35.3 %collective-permute-start.4 = (bf16[16,128,256]{2,1,0:T(8,128)(2,1)S(1)}, bf16[16,128,256]{2,1,0:T(8,128)(2,1)}, u32[]{:S(2)}, u32[]{:S(2)}) collective-permute-start(bf16[16,128,256]{2,1,0:T(8,128)(2,1)S(1)} %bitcast.26), channel_id=1, source_target_pairs={{0,112},{8,24},{16,0},{24,40},{32,16},{40,56},{48,32},{56,72},{64,... | collective-permute-start | bytes 3145736 | tf_op jit(solution)/shard_map/ppermute | solution.py:221
  20.3 28.0 %collective-permute-start = (bf16[16,128,256]{2,1,0:T(8,128)(2,1)S(1)}, bf16[16,128,256]{2,1,0:T(8,128)(2,1)}, u32[]{:S(2)}, u32[]{:S(2)}) collective-permute-start(bf16[16,128,256]{2,1,0:T(8,128)(2,1)S(1)} %bitcast.27), channel_id=1, source_target_pairs={{0,16},{8,120},{16,32},{24,8},{32,48},{40,24},{48,64},{56,40},{64,... | collective-permute-start | bytes 3145736 | tf_op jit(solution)/shard_map/ppermute | solution.py:221
  28.0 31.1 %all-to-all-start = ((bf16[32,8,1280]{2,0,1:T(8,128)(2,1)}), bf16[32,8,1280]{2,0,1:T(8,128)(2,1)S(1)}, u32[]{:S(2)}, u32[]{:S(2)}) async-start(bf16[32,8,1280]{2,0,1:T(8,128)(2,1)} %pad_maximum_fusion), calls=%async_computation | async-start | bytes 1310720 | tf_op jit(solution)/shard_map/all_to_all | solution.py:242
  48.3 26.2 %collective-permute-start.1 = (bf16[16,128,256]{2,1,0:T(8,128)(2,1)}, bf16[16,128,256]{2,1,0:T(8,128)(2,1)}, u32[]{:S(2)}, u32[]{:S(2)}) collective-permute-start(bf16[16,128,256]{2,1,0:T(8,128)(2,1)} %collective-permute-done.refs_0_), channel_id=1, source_target_pairs={{0,16},{8,120},{16,32},{24,8},{32,48},{40,24},{48,64},{56,40},{64,... | collective-permute-start | bytes 3145736 | tf_op jit(solution)/shard_map/ppermute | solution.py:221
  53.6 33.2 %collective-permute-start.5 = (bf16[16,128,256]{2,1,0:T(8,128)(2,1)}, bf16[16,128,256]{2,1,0:T(8,128)(2,1)}, u32[]{:S(2)}, u32[]{:S(2)}) collective-permute-start(bf16[16,128,256]{2,1,0:T(8,128)(2,1)} %collective-permute-done.4.refs_1_), channel_id=1, source_target_pairs={{0,112},{8,24},{16,0},{24,40},{32,16},{40,56},{48,32},{56,72},{64,... | collective-permute-start | bytes 3145736 | tf_op jit(solution)/shard_map/ppermute | solution.py:221
  59.0 20.7 %copy-start = (s32[64,64]{1,0:T(8,128)S(1)}, s32[64,64]{1,0:T(8,128)}, u32[]{:S(2)}) copy-start(s32[64,64]{1,0:T(8,128)} %select_reduce_fusion.table) | copy-start | bytes 49156
  59.0 20.7 %copy-start.9 = (s32[6]{0:T(128)S(1)}, s32[6]{0:T(128)}, u32[]{:S(2)}) copy-start(s32[6]{0:T(128)} %stack.15.place) | copy-start | bytes 76
  59.1 31.3 %all-to-all-start.4 = ((bf16[8,2,128,256]{3,2,1,0:T(8,128)(2,1)}), bf16[8,2,128,256]{3,2,1,0:T(8,128)(2,1)S(1)}, u32[]{:S(2)}, u32[]{:S(2)}) async-start(bf16[8,2,128,256]{3,2,1,0:T(8,128)(2,1)} %shard_map.69), calls=%async_computation.4 | async-start | bytes 2097152 | tf_op jit(solution)/shard_map/all_to_all | solution.py:224
  74.5 35.2 %collective-permute-start.2 = (bf16[16,128,256]{2,1,0:T(8,128)(2,1)}, bf16[16,128,256]{2,1,0:T(8,128)(2,1)}, u32[]{:S(2)}, u32[]{:S(2)}) collective-permute-start(bf16[16,128,256]{2,1,0:T(8,128)(2,1)} %collective-permute-done.1.refs_0_), channel_id=1, source_target_pairs={{0,16},{8,120},{16,32},{24,8},{32,48},{40,24},{48,64},{56,40},{64,... | collective-permute-start | bytes 3145736 | tf_op jit(solution)/shard_map/ppermute | solution.py:221
  85.8 1.0 copy-start.3
  90.4 23.5 %all-to-all-start.3 = ((bf16[8,2,128,256]{3,2,1,0:T(8,128)(2,1)}), bf16[8,2,128,256]{3,2,1,0:T(8,128)(2,1)S(1)}, u32[]{:S(2)}, u32[]{:S(2)}) async-start(bf16[8,2,128,256]{3,2,1,0:T(8,128)(2,1)} %shard_map.67), calls=%async_computation.3 | async-start | bytes 2097152 | tf_op jit(solution)/shard_map/all_to_all | solution.py:224
  95.0 5.3 %copy-start.1 = (s32[64,64]{1,0:T(8,128)S(1)}, s32[64,64]{1,0:T(8,128)}, u32[]{:S(2)}) copy-start(s32[64,64]{1,0:T(8,128)} %select_reduce_fusion.table) | copy-start | bytes 49156
  95.0 5.3 %copy-start.10 = (s32[6]{0:T(128)S(1)}, s32[6]{0:T(128)}, u32[]{:S(2)}) copy-start(s32[6]{0:T(128)} %stack.15.place) | copy-start | bytes 76
  98.3 11.3 %collective-permute-start.6 = (bf16[8,1,128,256]{3,2,0,1:T(8,128)(2,1)}, bf16[8,1,128,256]{3,2,0,1:T(8,128)(2,1)S(1)}, u32[]{:S(2)}, u32[]{:S(2)}) collective-permute-start(bf16[8,1,128,256]{3,2,0,1:T(8,128)(2,1)} %bitcast.29), channel_id=1, source_target_pairs={{0,112},{8,24},{16,0},{24,40},{32,16},{40,56},{48,32},{56,72},{64,... | collective-permute-start | bytes 1572872 | tf_op jit(solution)/shard_map/ppermute | solution.py:221
  100.3 1.2 copy-start.4
  106.5 1.0 copy-start.7
  109.7 0.8 copy-start.15
  113.9 21.2 %all-to-all-start.5 = ((bf16[8,2,128,256]{3,2,1,0:T(8,128)(2,1)}), bf16[8,2,128,256]{3,2,1,0:T(8,128)(2,1)S(1)}, u32[]{:S(2)}, u32[]{:S(2)}) async-start(bf16[8,2,128,256]{3,2,1,0:T(8,128)(2,1)} %shard_map.71), calls=%async_computation.5 | async-start | bytes 2097152 | tf_op jit(solution)/shard_map/all_to_all | solution.py:224
  120.5 21.4 %copy-start.2 = (s32[64,64]{1,0:T(8,128)S(1)}, s32[64,64]{1,0:T(8,128)}, u32[]{:S(2)}) copy-start(s32[64,64]{1,0:T(8,128)} %select_reduce_fusion.table) | copy-start | bytes 49156
  120.5 21.4 %copy-start.11 = (s32[6]{0:T(128)S(1)}, s32[6]{0:T(128)}, u32[]{:S(2)}) copy-start(s32[6]{0:T(128)} %stack.15.place) | copy-start | bytes 76
  123.7 10.6 %collective-permute-start.3 = (bf16[8,1,128,256]{3,2,1,0:T(8,128)(2,1)}, bf16[8,1,128,256]{3,2,1,0:T(8,128)(2,1)S(1)}, u32[]{:S(2)}, u32[]{:S(2)}) collective-permute-start(bf16[8,1,128,256]{3,2,1,0:T(8,128)(2,1)} %shard_map.66), channel_id=1, source_target_pairs={{0,16},{8,120},{16,32},{24,8},{32,48},{40,24},{48,64},{56,40},{64,... | collective-permute-start | bytes 1572872 | tf_op jit(solution)/shard_map/ppermute | solution.py:221
  134.3 0.8 copy-start.14
  135.1 21.8 %all-to-all-start.2 = ((bf16[8,1,128,256]{3,2,1,0:T(8,128)(2,1)}), bf16[8,1,128,256]{3,2,1,0:T(8,128)(2,1)S(1)}, u32[]{:S(2)}, u32[]{:S(2)}) async-start(bf16[8,1,128,256]{3,2,1,0:T(8,128)(2,1)} %copy-done.14), calls=%async_computation.2 | async-start | bytes 1048576 | tf_op jit(solution)/shard_map/all_to_all | solution.py:224
  141.9 1.2 copy-start.8
  155.9 1.0 copy-start.5
  156.9 1.2 copy-start.6

commit v2 on v1

v2 whole, which is shorter than its diff:
```python
import functools
import math

import jax
import jax.numpy as jnp
from jax import lax
from jax.experimental import pallas as pl
from jax.experimental.pallas import tpu as pltpu
from jax.sharding import Mesh
from jax.sharding import PartitionSpec as P

QH = 64
KVH = 8
GROUP = QH // KVH
MASKED_SCORE = -1e30
PEERS = 8
PLANE = ("core", "pool")
ANY = pl.BlockSpec(memory_space=pltpu.HBM)
VMEM = pl.BlockSpec(memory_space=pltpu.VMEM)


def cost_of(microseconds):
    return pl.CostEstimate(
        flops=int(microseconds * 1.1e9), transcendentals=0, bytes_accessed=int(microseconds * 3.6e6)
    )


def pick_kernel(outputs, count, place, table, *refs):
    buffers, outs, sem = refs[:count], refs[-1 - len(outputs) : -1], refs[-1]
    x, z, c = place[0], place[1], place[2]
    planes, cores = place[4], place[5]
    way = 1 - 2 * c
    copies = []
    for out, columns in zip(outs, outputs):
        peers = out.shape[0]
        pools = peers // 2
        for column, (buffer, request_step, owner_step) in enumerate(columns):
            request_z = lax.rem(z + request_step * way + planes, planes)
            owner_z = lax.rem(z + owner_step * way + planes, planes)
            owner = (x * planes + owner_z) * cores + c
            for peer in range(peers):
                request = (peer % pools * planes + request_z) * cores + peer // pools
                slot = jnp.maximum(table[request, owner] - 1, 0)
                copy = pltpu.make_async_copy(buffers[buffer].at[slot], out.at[peer, column], sem)
                copy.start()
                copies.append(copy)
    for copy in copies:
        copy.wait()


def pick(place, table, buffers, outputs, peers, after=(), cost=4):
    block, dtype = buffers[0].shape[1:], buffers[0].dtype
    operands = list(buffers) + list(after)
    return pl.pallas_call(
        functools.partial(pick_kernel, outputs, len(buffers)),
        grid_spec=pltpu.PrefetchScalarGridSpec(
            num_scalar_prefetch=2,
            grid=(1,),
            in_specs=[ANY] * len(operands),
            out_specs=[pl.BlockSpec((peers, len(columns)) + block, lambda *_: (0, 0, 0, 0)) for columns in outputs],
            scratch_shapes=[pltpu.SemaphoreType.DMA],
        ),
        out_shape=[jax.ShapeDtypeStruct((peers, len(columns)) + block, dtype) for columns in outputs],
        cost_estimate=cost_of(cost),
    )(place, table, *operands)


def join_kernel(*refs):
    arrays, out, sem = refs[:-2], refs[-2], refs[-1]
    copies = [pltpu.make_async_copy(array, out.at[:, at : at + 1], sem) for at, array in enumerate(arrays)]
    for copy in copies:
        copy.start()
    for copy in copies:
        copy.wait()


def join(arrays, cost):
    peers, _, *block = arrays[0].shape
    shape = (peers, len(arrays), *block)
    return pl.pallas_call(
        join_kernel,
        grid=(1,),
        in_specs=[ANY] * len(arrays),
        out_specs=pl.BlockSpec(shape, lambda _: (0, 0, 0, 0)),
        scratch_shapes=[pltpu.SemaphoreType.DMA],
        out_shape=jax.ShapeDtypeStruct(shape, arrays[0].dtype),
        cost_estimate=cost_of(cost),
    )(*arrays)


def attend_kernel(rounds, chunk, first, last, scale, spare_operands, place, table, *refs):
    refs = list(refs)
    q_in = refs.pop(0)
    arrived = [refs.pop(0) for _ in rounds]
    if not first:
        acc_in, ml_in = refs.pop(0), refs.pop(0)
    del refs[:spare_operands]
    if last:
        out_ref = refs.pop(0)
    else:
        acc_out, ml_out = refs.pop(0), refs.pop(0)
    if first:
        turned_out = refs.pop(0)
    blocks, acc, ml, query_buffer, turned, sem, state_sem = refs
    x, z, c = place[0], place[1], place[2]
    pools, planes, cores = place[3], place[4], place[5]
    me = (x * planes + z) * cores + c
    group, head_dim, tokens = acc.shape
    block_len = arrived[0].shape[2]
    if first:
        loads = [pltpu.make_async_copy(q_in, query_buffer, state_sem)]
    else:
        pairs = ((q_in, turned), (acc_in, acc), (ml_in, ml))
        loads = [pltpu.make_async_copy(source, target, state_sem) for source, target in pairs]
    for load in loads:
        load.start()

    def fetch(source, at):
        return pltpu.make_async_copy(source, blocks.at[pl.ds(at * block_len, block_len)], sem)

    count = jnp.int32(0)
    for array, (start, steps) in zip(arrived, rounds):
        for lane in range(array.shape[0]):
            core, sender = divmod(start + lane, PEERS // 2)
            way = 1 - 2 * core
            for column in range(array.shape[1]):
                if steps[column] is None:
                    continue
                owner_z = lax.rem(z + steps[column] * way + planes, planes)
                live = table[me, (sender * planes + owner_z) * cores + core] > 0

                @pl.when(live)
                def _():
                    fetch(array.at[lane, column], count).start()

                count = count + live.astype(jnp.int32)
    chunks = (count + chunk - 1) // chunk
    spare = arrived[0].at[0, 0]

    def fill(at, carried):
        fetch(spare, at).start()
        return carried

    def drain(at, carried):
        fetch(spare, at).wait()
        return carried

    lax.fori_loop(count, chunks * chunk, fill, 0)

    def scores_of(head, keys):
        query = turned[head * head_dim : (head + 1) * head_dim, :]
        return jnp.dot(keys, query, preferred_element_type=jnp.float32)

    def absorb(pending):
        head, weights, values, shrink = pending
        add = jnp.dot(values, weights, preferred_element_type=jnp.float32)
        acc[head] = add if shrink is None else acc[head] * shrink + add

    def sweep(keys, values, mask, fresh):
        score, pending = scores_of(0, keys), None
        for head in range(group):
            ahead = scores_of(head + 1, keys) if head + 1 < group else None
            score = mask(score)
            top = jnp.max(score, axis=0, keepdims=True)
            shrink = None
            if not fresh:
                old = ml[0, head : head + 1, :]
                top = jnp.maximum(top, old)
                shrink = jnp.exp2((old - top) * scale)
            weights = jnp.exp2((score - top) * scale)
            total = jnp.sum(weights, axis=0, keepdims=True)
            ml[1, head : head + 1, :] = total if fresh else ml[1, head : head + 1, :] * shrink + total
            ml[0, head : head + 1, :] = top
            if pending is not None:
                absorb(pending)
            pending = (head, weights.astype(values.dtype), values, shrink)
            score = ahead
        absorb(pending)

    for load in loads:
        load.wait()
    if first:
        turned[...] = query_buffer[:, : group * head_dim].T
        own = query_buffer[:, group * head_dim :]
        key = lax.broadcasted_iota(jnp.int32, (tokens, tokens), 0)
        token = lax.broadcasted_iota(jnp.int32, (tokens, tokens), 1)
        sweep(own[:, :head_dim], own[:, head_dim:].T, lambda s: jnp.where(key <= token, s, MASKED_SCORE), True)
    lax.fori_loop(0, chunks * chunk, drain, 0)

    def body(at, carried):
        size = chunk * block_len
        kv = blocks[pl.ds(pl.multiple_of(at * size, size), size), :]

        def mask(score):
            parts = [score[:block_len]]
            for b in range(1, chunk):
                part = score[b * block_len : (b + 1) * block_len]
                parts.append(jnp.where(at * chunk + b < count, part, MASKED_SCORE))
            return jnp.concatenate(parts, axis=0)

        sweep(kv[:, :head_dim], kv[:, head_dim:].T, mask, False)
        return carried

    lax.fori_loop(0, chunks, body, 0)
    if last:
        for head in range(group):
            done = acc[head] / ml[1, head : head + 1, :]
            out_ref[:, head * head_dim : (head + 1) * head_dim] = done.T.astype(out_ref.dtype)
    else:
        pairs = [(acc, acc_out), (ml, ml_out)] + ([(turned, turned_out)] if first else [])
        stores = [pltpu.make_async_copy(source, target, state_sem) for source, target in pairs]
        for store in stores:
            store.start()
        for store in stores:
            store.wait()


def attend(place, table, query, arrived, rounds, state, last, scale, group, head_dim, tokens, after=(), cost=8, chunk=8):
    first = state is None
    dtype = arrived[0].dtype
    slots = sum(array.shape[0] * array.shape[1] for array in arrived)
    slots = (slots + chunk - 1) // chunk * chunk
    block_len = arrived[0].shape[2]
    operands = [query] + list(arrived) + ([] if first else list(state)) + list(after)
    acc = ((group, head_dim, tokens), jnp.float32)
    ml = ((2, group, tokens), jnp.float32)
    turned = ((group * head_dim, tokens), dtype)
    outs = [((tokens, group * head_dim), dtype)] if last else [acc, ml]
    if first:
        outs.append(turned)
    return pl.pallas_call(
        functools.partial(
            attend_kernel, rounds, chunk, first, last, scale * math.log2(math.e), len(after)
        ),
        grid_spec=pltpu.PrefetchScalarGridSpec(
            num_scalar_prefetch=2,
            grid=(1,),
            in_specs=[ANY] * len(operands),
            out_specs=[VMEM if last else ANY] * len(outs),
            scratch_shapes=[
                pltpu.VMEM((slots * block_len, 2 * head_dim), dtype),
                pltpu.VMEM(*acc),
                pltpu.VMEM(*ml),
                pltpu.VMEM(query.shape if first else (16, 128), dtype),
                pltpu.VMEM(*turned),
                pltpu.SemaphoreType.DMA,
                pltpu.SemaphoreType.DMA,
            ],
        ),
        out_shape=[jax.ShapeDtypeStruct(*out) for out in outs],
        compiler_params=pltpu.CompilerParams(vmem_limit_bytes=20 * 1024 * 1024),
        cost_estimate=cost_of(cost),
    )(place, table, *operands)


def local(queries, stretch_kv, pool_kv, prefix_blocks, block_owner, block_slot):
    pools, planes, cores = lax.axis_size("pool"), lax.axis_size("z"), lax.axis_size("core")
    x, z, c = lax.axis_index("pool"), lax.axis_index("z"), lax.axis_index("core")
    tensor_count = lax.axis_size("tp")
    owner_count = pools * planes * cores
    peers = pools * cores
    tok_local = queries.shape[1]
    block_len, pair = pool_kv.shape[1], pool_kv.shape[3]
    head_dim = pair // 2
    scale = 1.0 / math.sqrt(head_dim)
    max_blocks = block_owner.shape[1]
    pool = pool_kv.reshape(-1, block_len, pair)

    def hop(array, step, mirrored):
        pairs = []
        for at in range(planes):
            for core in range(cores):
                way = -step if mirrored and core else step
                pairs.append((at * cores + core, (at + way) % planes * cores + core))
        return lax.ppermute(array, ("z", "core"), pairs)

    def deliver(array):
        return lax.all_to_all(array, PLANE, split_axis=0, concat_axis=0, tiled=True)

    long1, short1 = hop(pool, 1, True), hop(pool, -1, True)

    where = (x, z, c, pools, planes, cores)
    place = jnp.stack([jnp.int32(value) for value in where])
    position = jnp.arange(max_blocks, dtype=jnp.int32)
    live = position[None, :] < prefix_blocks[:, None]
    owners = jnp.arange(owner_count, dtype=jnp.int32)
    table = jnp.sum(
        jnp.where(
            (block_owner[:, :, None] == owners[None, None, :]) & live[:, :, None],
            block_slot[:, :, None] + 1,
            0,
        ),
        axis=1,
    )

    both = jnp.concatenate([queries[0].reshape(tok_local, tensor_count, -1), stretch_kv[0]], axis=2)
    q_kv = lax.all_to_all(both, "tp", split_axis=1, concat_axis=0, tiled=True)
    tokens = tok_local * tensor_count
    q_kv = q_kv.reshape(tokens, -1)
    get = functools.partial(pick, place, table, peers=peers)
    step = functools.partial(
        attend, place, table, scale=scale, group=GROUP, head_dim=head_dim, tokens=tokens
    )
    long2, short2 = hop(long1, 1, True), hop(short1, -1, True)
    half_peers = peers // 2
    (start,) = get([pool], (((0, 4, 0), (0, 0, 0)),))
    start, q_kv = lax.optimization_barrier((start, q_kv))
    start = deliver(start)
    (send_near,) = get([long1, short1], (((0, 0, -1), (1, 0, 1)),))
    near = deliver(send_near)
    *state, query = step(q_kv, [start], ((0, (None, 0)),), None, False, after=[send_near])
    send_long, send_short = get([long2, short2], (((0, 1, -2),), ((1, -1, 2),)), after=[state[0]])
    long3, short3 = hop(send_long, 1, True), hop(send_short, -1, True)
    (middle_sent,) = get([long2, short2], (((0, 0, -2), (1, 0, 2)),), after=[send_long])
    middle = deliver(middle_sent)
    state = step(query, [near], ((0, (-1, 1)),), state, False, after=[middle_sent])
    far, long3 = lax.optimization_barrier((start, long3))
    far_up, far_down = hop(far[:half_peers, :1], 4, False), hop(far[half_peers:, :1], -4, False)
    third = join([long3, short3], cost=30)
    state = step(query, [middle], ((0, (-2, 2)),), state, False, after=[third], cost=10)
    third = deliver(third)
    (attended,) = step(
        query, [third, far_up, far_down], ((0, (-3, 3)), (0, (4,)), (half_peers, (4,))), state, True
    )
    attended = attended.reshape(tensor_count, tok_local, -1)
    return lax.all_to_all(attended, "tp", split_axis=0, concat_axis=2, tiled=True)


def solution(mesh):
    pools, seq, tensor = mesh.devices.shape
    fine = Mesh(mesh.devices.reshape(pools, seq // 2, 2, tensor), ("pool", "z", "core", "tp"))
    rows = ("pool", "z", "core")
    return jax.shard_map(
        local,
        mesh=fine,
        in_specs=(
            P(rows, "tp", None),
            P(rows, "tp", None, None),
            P(rows, None, "tp", None),
            P(),
            P(),
            P(),
        ),
        out_specs=P(rows, "tp", None),
        check_vma=False,
    )
```

time: 191 us -> 177 us (0.927)
  waiting for transfers between devices: 33.1 us -> 10.6 us
  local copies, waits for them, and re-layouts: 11.2 us -> 19.4 us
  Pallas kernels: 49.3 us -> 53.4 us
    ppermute x7 -> x8, waiting for transfers between devices: 33 us -> 8.24 us  [hop(): return lax.ppermute(array, ('z', 'core'), pairs)]
    all_to_all x5 -> x4, starting transfers between devices: 32.3 us -> 21.5 us  [deliver(): return lax.all_to_all(array, PLANE, split_axis=0, concat_axis=0, tiled=True)]
    ppermute x7 -> x8, starting transfers between devices: 26.4 us -> 36.7 us  [hop(): return lax.ppermute(array, ('z', 'core'), pairs)]
    pallas_call x4, Pallas kernels: 29 us -> 37 us  [attend(): pl.pallas_call(functools.partial(attend_kernel, rounds, chunk, first, las...]
    unnamed x36 -> x48, local copies, waits for them, and re-layouts: 9.3 us -> 15.7 us
    pallas_call x6 -> x5, Pallas kernels: 20.3 us -> 16.4 us  [the longest x4 14.2 us: pick(): pl.pallas_call(functools.partial(pick_kernel, outputs, len(buffers)), gri...]
  transfers between devices with their start and end apart: 13 -> 13, of which waited for: 4 -> 5; matrix products, arithmetic and copies ran while one was open for 1% -> 2% of each run, Pallas kernels for 22% -> 23%
where the time goes in v2:
time: 177 us; the launch traced here: 175 us
  starting transfers between devices  65.2 us (37%)
  Pallas kernels  53.4 us (30%)
  blocking collectives  22.7 us (13%)
  local copies, waits for them, and re-layouts  19.4 us (11%)
  waiting for transfers between devices  10.6 us (6%)
  other arithmetic  3.32 us (2%)
    pallas_call x4, Pallas kernels, attend(): pl.pallas_call(functools.partial(attend_kernel, rounds, chunk, first, las...  37 us
    ppermute x8, starting transfers between devices, hop(): return lax.ppermute(array, ('z', 'core'), pairs)  36.7 us
    all_to_all x1, blocking collectives, local(): lax.all_to_all(attended, 'tp', split_axis=0, concat_axis=2, tiled=True)  22.7 us
    all_to_all x4, starting transfers between devices, deliver(): return lax.all_to_all(array, PLANE, split_axis=0, concat_axis=0, tiled=True)  21.5 us
    unnamed x48, local copies, waits for them, and re-layouts  15.7 us
    pallas_call x4, Pallas kernels, pick(): pl.pallas_call(functools.partial(pick_kernel, outputs, len(buffers)), gri...  14.2 us
    ppermute x8, waiting for transfers between devices, hop(): return lax.ppermute(array, ('z', 'core'), pairs)  8.24 us
    all_to_all x1, starting transfers between devices, local(): q_kv = lax.all_to_all(both, 'tp', split_axis=1, concat_axis=0, tiled=True)  6.95 us
  transfers between devices with their start and end apart: 13, of which 5 were waited for; matrix products, arithmetic and copies ran while one was open for 2% of the time, Pallas kernels for 23%

profile of v2, /device:TPU:7, one launch (start us, length us, event | category | flops | bytes accessed | tf_op | source)
XLA Modules:
  0.0 174.9 jit_solution(15844156839080272201)
XLA Ops:
  0.0 0.9 copy.15
  0.9 1.3 copy.18
  2.3 0.3 copy.14
  2.6 0.0 copy-start.22
  2.6 0.0 copy-start.20
  2.6 0.0 copy-start.19
  2.6 0.9 pad_maximum_fusion
  3.5 7.0 %all-to-all-start = ((bf16[32,8,1280]{2,0,1:T(8,128)(2,1)}), bf16[32,8,1280]{2,0,1:T(8,128)(2,1)S(1)}, u32[]{:S(2)}, u32[]{:S(2)}) async-start(bf16[32,8,1280]{2,0,1:T(8,128)(2,1)} %pad_maximum_fusion), calls=%async_computation | async-start | bytes 1310720 | tf_op jit(solution)/shard_map/all_to_all | solution.py:297
  10.5 4.0 %collective-permute-start.1 = (bf16[16,128,256]{2,1,0:T(8,128)(2,1)S(1)}, bf16[16,128,256]{2,1,0:T(8,128)(2,1)}, u32[]{:S(2)}, u32[]{:S(2)}) collective-permute-start(bf16[16,128,256]{2,1,0:T(8,128)(2,1)S(1)} %bitcast.26), channel_id=1, source_target_pairs={{0,112},{8,24},{16,0},{24,40},{32,16},{40,56},{48,32},{56,72},{64,... | collective-permute-start | bytes 3145736 | tf_op jit(solution)/shard_map/ppermute | solution.py:275
  14.5 8.6 %collective-permute-start = (bf16[16,128,256]{2,1,0:T(8,128)(2,1)S(1)}, bf16[16,128,256]{2,1,0:T(8,128)(2,1)}, u32[]{:S(2)}, u32[]{:S(2)}) collective-permute-start(bf16[16,128,256]{2,1,0:T(8,128)(2,1)S(1)} %bitcast.27), channel_id=1, source_target_pairs={{0,16},{8,120},{16,32},{24,8},{32,48},{40,24},{48,64},{56,40},{64,... | collective-permute-start | bytes 3145736 | tf_op jit(solution)/shard_map/ppermute | solution.py:275
  23.1 0.1 copy.13
  23.2 0.1 copy.12
  23.3 0.6 stack.15.place
  23.9 0.1 iota_compare_fusion.1
  24.0 2.3 %select_reduce_fusion.table = s32[64,64]{1,0:T(8,128)} fusion(s32[64,48]{1,0:T(8,128)S(1)} %copy.13, s32[64,48]{1,0:T(8,128)S(1)} %copy.12, pred[64,48]{1,0:T(8,128)(4,1)S(1)} %iota_compare_fusion.1), kind=kLoop, calls=%fused_computation | loop fusion | flops 782336 | bytes 44032 | tf_op jit(solution)/shard_map/reduce_sum | solution.py:287
  26.3 3.6 %shard_map.64 = bf16[8,2,128,256]{3,2,1,0:T(8,128)(2,1)} custom-call(s32[6]{0:T(128)} %stack.15.place, s32[64,64]{1,0:T(8,128)} %select_reduce_fusion.table, bf16[16,128,256]{2,1,0:T(8,128)(2,1)} %bitcast.25), custom_call_target="tpu_custom_call" | custom-call | flops 4400000000 | bytes 14400000 | tf_op jit(solution)/shard_map/pallas_call | solution.py:54
  30.0 1.3 all-to-all-done
  31.2 0.8 copy-done.3
  32.1 4.9 %all-to-all-start.1 = ((bf16[8,2,128,256]{3,2,1,0:T(8,128)(2,1)}), bf16[8,2,128,256]{3,2,1,0:T(8,128)(2,1)S(1)}, u32[]{:S(2)}, u32[]{:S(2)}) async-start(bf16[8,2,128,256]{3,2,1,0:T(8,128)(2,1)} %shard_map.64), calls=%async_computation.1 | async-start | bytes 2097152 | tf_op jit(solution)/shard_map/all_to_all | solution.py:278
  37.0 1.6 collective-permute-done.1.refs_1_
  38.6 2.4 %collective-permute-start.3 = (bf16[16,128,256]{2,1,0:T(8,128)(2,1)}, bf16[16,128,256]{2,1,0:T(8,128)(2,1)}, u32[]{:S(2)}, u32[]{:S(2)}) collective-permute-start(bf16[16,128,256]{2,1,0:T(8,128)(2,1)} %collective-permute-done.1.refs_1_), channel_id=1, source_target_pairs={{0,112},{8,24},{16,0},{24,40},{32,16},{40,56},{48,32},{56,72},{64,... | collective-permute-start | bytes 3145736 | tf_op jit(solution)/shard_map/ppermute | solution.py:275
  41.0 4.5 %collective-permute-done.refs_0_ = bf16[16,128,256]{2,1,0:T(8,128)(2,1)} collective-permute-done((bf16[16,128,256]{2,1,0:T(8,128)(2,1)S(1)}, bf16[16,128,256]{2,1,0:T(8,128)(2,1)}, u32[]{:S(2)}, u32[]{:S(2)}) %collective-permute-start) | collective-permute-done | bytes 1048608 | tf_op jit(solution)/shard_map/ppermute | solution.py:275
  45.5 5.3 %collective-permute-start.2 = (bf16[16,128,256]{2,1,0:T(8,128)(2,1)}, bf16[16,128,256]{2,1,0:T(8,128)(2,1)}, u32[]{:S(2)}, u32[]{:S(2)}) collective-permute-start(bf16[16,128,256]{2,1,0:T(8,128)(2,1)} %collective-permute-done.refs_0_), channel_id=1, source_target_pairs={{0,16},{8,120},{16,32},{24,8},{32,48},{40,24},{48,64},{56,40},{64,... | collective-permute-start | bytes 3145736 | tf_op jit(solution)/shard_map/ppermute | solution.py:275
  50.8 3.5 %shard_map.65.refs_2_ = bf16[8,2,128,256]{3,2,1,0:T(8,128)(2,1)} custom-call(s32[6]{0:T(128)} %stack.15.place, s32[64,64]{1,0:T(8,128)} %select_reduce_fusion.table, bf16[16,128,256]{2,1,0:T(8,128)(2,1)} %collective-permute-done.refs_0_, bf16[16,128,256]{2,1,0:T(8,128)(2,1)} %collective-permute-done.1.refs_1_), custom_call_target="tpu_custom_call" | custom-call | flops 4400000000 | bytes 14400000 | tf_op jit(solution)/shard_map/pallas_call | solution.py:54
  54.4 0.0 all-to-all-done.1.refs_1_
  54.4 6.6 %all-to-all-start.4 = ((bf16[8,2,128,256]{3,2,1,0:T(8,128)(2,1)}), bf16[8,2,128,256]{3,2,1,0:T(8,128)(2,1)S(1)}, u32[]{:S(2)}, u32[]{:S(2)}) async-start(bf16[8,2,128,256]{3,2,1,0:T(8,128)(2,1)} %shard_map.65.refs_2_), calls=%async_computation.4 | async-start | bytes 2097152 | tf_op jit(solution)/shard_map/all_to_all | solution.py:278
  61.1 1.2 copy-done.1
  62.3 1.1 copy-done.4
  63.4 6.4 %shard_map.66 = (f32[8,128,256]{2,1,0:T(8,128)S(1)}, f32[2,8,256]{2,1,0:T(8,128)S(1)}, bf16[1024,256]{1,0:T(8,128)(2,1)S(1)}) custom-call(s32[6]{0:T(128)S(1)} %copy-done.7, s32[64,64]{1,0:T(8,128)S(1)} %copy-done.5, bf16[256,1280]{1,0:T(8,128)(2,1)S(1)} %bitcast.19, bf16[8,2,128,256]{3,2,1,0:T(8,128)(2,1)S(1)} %all-to-all-done.1.refs_1_, ...), custom_call_target="tpu_custom_call" | custom-call | flops 8800000000 | bytes 28800000 | tf_op jit(solution)/shard_map/pallas_call | solution.py:231
  69.8 1.0 copy-done.9
  70.8 0.8 copy-done.15
  71.6 0.0 collective-permute-done.3.refs_1_
  71.6 2.1 %collective-permute-done.2.refs_0_ = bf16[16,128,256]{2,1,0:T(8,128)(2,1)} collective-permute-done((bf16[16,128,256]{2,1,0:T(8,128)(2,1)}, bf16[16,128,256]{2,1,0:T(8,128)(2,1)}, u32[]{:S(2)}, u32[]{:S(2)}) %collective-permute-start.2) | collective-permute-done | bytes 1048608 | tf_op jit(solution)/shard_map/ppermute | solution.py:275
  73.7 3.5 %shard_map.67 = (bf16[8,1,128,256]{3,2,1,0:T(8,128)(2,1)}, bf16[8,1,128,256]{3,2,1,0:T(8,128)(2,1)}) custom-call(s32[6]{0:T(128)} %stack.15.place, s32[64,64]{1,0:T(8,128)} %select_reduce_fusion.table, bf16[16,128,256]{2,1,0:T(8,128)(2,1)} %collective-permute-done.2.refs_0_, bf16[16,128,256]{2,1,0:T(8,128)(2,1)} %collective-permute-done.3.refs_1_, ...), custom_call_target="tpu_custom_call" | custom-call | flops 4400000000 | bytes 14400000 | tf_op jit(solution)/shard_map/pallas_call | solution.py:54
  77.1 1.9 %collective-permute-start.5 = (bf16[8,1,128,256]{3,2,1,0:T(8,128)(2,1)}, bf16[8,1,128,256]{3,2,1,0:T(8,128)(2,1)}, u32[]{:S(2)}, u32[]{:S(2)}) collective-permute-start(bf16[8,1,128,256]{3,2,1,0:T(8,128)(2,1)} %get-tuple-element.24), channel_id=1, source_target_pairs={{0,112},{8,24},{16,0},{24,40},{32,16},{40,56},{48,32},{56,72},{64,... | collective-permute-start | bytes 1572872 | tf_op jit(solution)/shard_map/ppermute | solution.py:275
  79.1 5.3 %collective-permute-start.4 = (bf16[8,1,128,256]{3,2,1,0:T(8,128)(2,1)}, bf16[8,1,128,256]{3,2,1,0:T(8,128)(2,1)}, u32[]{:S(2)}, u32[]{:S(2)}) collective-permute-start(bf16[8,1,128,256]{3,2,1,0:T(8,128)(2,1)} %get-tuple-element.22.refs_2_), channel_id=1, source_target_pairs={{0,16},{8,120},{16,32},{24,8},{32,48},{40,24},{48,64},{56,40},{64,... | collective-permute-start | bytes 1572872 | tf_op jit(solution)/shard_map/ppermute | solution.py:275
  84.4 3.6 %shard_map.69.refs_4_ = bf16[8,2,128,256]{3,2,1,0:T(8,128)(2,1)} custom-call(s32[6]{0:T(128)} %stack.15.place, s32[64,64]{1,0:T(8,128)} %select_reduce_fusion.table, bf16[16,128,256]{2,1,0:T(8,128)(2,1)} %collective-permute-done.2.refs_0_, bf16[16,128,256]{2,1,0:T(8,128)(2,1)} %collective-permute-done.3.refs_1_, ...), custom_call_target="tpu_custom_call" | custom-call | flops 4400000000 | bytes 14400000 | tf_op jit(solution)/shard_map/pallas_call | solution.py:54
  88.0 0.0 all-to-all-done.4.refs_1_
  88.0 5.3 %all-to-all-start.3 = ((bf16[8,2,128,256]{3,2,1,0:T(8,128)(2,1)}), bf16[8,2,128,256]{3,2,1,0:T(8,128)(2,1)S(1)}, u32[]{:S(2)}, u32[]{:S(2)}) async-start(bf16[8,2,128,256]{3,2,1,0:T(8,128)(2,1)} %shard_map.69.refs_4_), calls=%async_computation.3 | async-start | bytes 2097152 | tf_op jit(solution)/shard_map/all_to_all | solution.py:278
  93.3 1.2 copy-done
  94.6 1.2 copy-done.10
  95.8 1.0 copy-done.16
  96.8 8.9 %shard_map.70 = (f32[8,128,256]{2,1,0:T(8,128)S(1)}, f32[2,8,256]{2,1,0:T(8,128)S(1)}) custom-call(s32[6]{0:T(128)S(1)} %copy-done.8, s32[64,64]{1,0:T(8,128)S(1)} %copy-done.6, bf16[1024,256]{1,0:T(8,128)(2,1)S(1)} %copy-done.16, bf16[8,2,128,256]{3,2,1,0:T(8,128)(2,1)S(1)} %all-to-all-done.4.refs_1_, f32[8,128,256]{2,1,0:T(8,128)S(1)} %copy-done.10, ...), custom_call_target="tpu_custom_call" | custom-call | flops 8800000000 | bytes 28800000 | tf_op jit(solution)/shard_map/pallas_call | solution.py:231
  105.7 0.0 collective-permute-done.4.refs_0_
  105.8 0.9 fusion.1
  106.7 0.2 copy-done.11
  106.9 1.9 %collective-permute-start.7 = (bf16[4,1,128,256]{3,2,1,0:T(8,128)(2,1)}, bf16[4,1,128,256]{3,2,1,0:T(8,128)(2,1)S(1)}, u32[]{:S(2)}, u32[]{:S(2)}) collective-permute-start(bf16[4,1,128,256]{3,2,1,0:T(8,128)(2,1)} %get-tuple-element.31), channel_id=1, source_target_pairs={{0,64},{8,72},{16,80},{24,88},{32,96},{40,104},{48,112},{56,120},{... | collective-permute-start | bytes 786440 | tf_op jit(solution)/shard_map/ppermute | solution.py:275
  108.8 7.3 %collective-permute-start.6 = (bf16[4,1,128,256]{3,2,1,0:T(8,128)(2,1)}, bf16[4,1,128,256]{3,2,1,0:T(8,128)(2,1)}, u32[]{:S(2)}, u32[]{:S(2)}) collective-permute-start(bf16[4,1,128,256]{3,2,1,0:T(8,128)(2,1)} %get-tuple-element.32), channel_id=1, source_target_pairs={{0,64},{8,72},{16,80},{24,88},{32,96},{40,104},{48,112},{56,120},{... | collective-permute-start | bytes 786440 | tf_op jit(solution)/shard_map/ppermute | solution.py:275
  116.1 0.0 collective-permute-done.5.refs_1_
  116.1 2.2 %shard_map.68.refs_4_ = bf16[8,2,128,256]{3,2,1,0:T(8,128)(2,1)} custom-call(bf16[8,1,128,256]{3,2,1,0:T(8,128)(2,1)} %collective-permute-done.4.refs_0_, bf16[8,1,128,256]{3,2,1,0:T(8,128)(2,1)} %collective-permute-done.5.refs_1_), custom_call_target="tpu_custom_call" | custom-call | flops 32999999488 | bytes 108000000 | tf_op jit(solution)/shard_map/pallas_call | solution.py:80
  118.3 0.0 all-to-all-done.3.refs_1_
  118.4 4.7 %all-to-all-start.2 = ((bf16[8,2,128,256]{3,2,1,0:T(8,128)(2,1)}), bf16[8,2,128,256]{3,2,1,0:T(8,128)(2,1)S(1)}, u32[]{:S(2)}, u32[]{:S(2)}) async-start(bf16[8,2,128,256]{3,2,1,0:T(8,128)(2,1)} %shard_map.68.refs_4_), calls=%async_computation.2 | async-start | bytes 2097152 | tf_op jit(solution)/shard_map/all_to_all | solution.py:278
  123.0 1.2 copy-done.12
  124.3 1.0 copy-done.17
  125.3 9.1 %shard_map.71 = (f32[8,128,256]{2,1,0:T(8,128)S(1)}, f32[2,8,256]{2,1,0:T(8,128)S(1)}) custom-call(s32[6]{0:T(128)S(1)} %copy-done.8, s32[64,64]{1,0:T(8,128)S(1)} %copy-done.6, bf16[1024,256]{1,0:T(8,128)(2,1)S(1)} %copy-done.17, bf16[8,2,128,256]{3,2,1,0:T(8,128)(2,1)S(1)} %all-to-all-done.3.refs_1_, f32[8,128,256]{2,1,0:T(8,128)S(1)} %copy-done.12, ...), custom_call_target="tpu_custom_call" | custom-call | flops 11000000512 | bytes 36000000 | tf_op jit(solution)/shard_map/pallas_call | solution.py:231
  134.4 1.0 copy-done.13
  135.4 0.0 collective-permute-done.7.refs_3_
  135.4 0.0 collective-permute-done.6.refs_2_
  135.4 1.1 all-to-all-done.2.refs_1_
  136.4 1.2 copy-done.14
  137.7 1.0 copy-done.18
  138.7 12.6 %shard_map.72 = bf16[256,1024]{1,0:T(8,128)(2,1)S(1)} custom-call(s32[6]{0:T(128)S(1)} %copy-done.8, s32[64,64]{1,0:T(8,128)S(1)} %copy-done.6, bf16[1024,256]{1,0:T(8,128)(2,1)S(1)} %copy-done.18, bf16[8,2,128,256]{3,2,1,0:T(8,128)(2,1)S(1)} %all-to-all-done.2.refs_1_, bf16[4,1,128,256]{3,2,1,0:T(8,128)(2,1)} %collective-permute-done.6.refs_2_, ...), custom_call_target="tpu_custom_call" | custom-call | flops 8800000000 | bytes 28800000 | tf_op jit(solution)/shard_map/pallas_call | solution.py:231
  151.3 22.7 %all_to_all.53 = bf16[8,32,1024]{2,1,0:T(8,128)(2,1)S(1)} all-to-all(bf16[8,32,1024]{2,1,0:T(8,128)(2,1)S(1)} %bitcast.20), channel_id=1, replica_groups=mesh['pool'=4,'z'=8,'core'=2,'tp'=8] {'tp'}, dimensions={0} | all-to-all | bytes 1048576 | tf_op jit(solution)/shard_map/all_to_all | solution.py:326
  174.0 0.8 copy.17
  (30 shorter events, 0.1 us)
Async XLA Ops:
  2.6 7.9 %copy-start.22 = (bf16[16,128,1,256]{3,1,2,0:T(8,128)(2,1)S(1)}, bf16[16,128,1,256]{3,1,2,0:T(8,128)(2,1)}, u32[]{:S(2)}) copy-start(bf16[16,128,1,256]{3,1,2,0:T(8,128)(2,1)} %param.8) | copy-start | bytes 3145732
  2.6 20.5 %copy-start.20 = (s32[64,48]{0,1:T(8,128)S(1)}, s32[64,48]{0,1:T(8,128)}, u32[]{:S(2)}) copy-start(s32[64,48]{0,1:T(8,128)} %param.11) | copy-start | bytes 36868
  2.6 20.6 %copy-start.19 = (s32[64,48]{0,1:T(8,128)S(1)}, s32[64,48]{0,1:T(8,128)}, u32[]{:S(2)}) copy-start(s32[64,48]{0,1:T(8,128)} %param.10) | copy-start | bytes 36868
  3.5 20.4 %copy-start.21 = (s32[64]{0:T(128)S(1)}, s32[64]{0:T(128)}, u32[]{:S(2)}) copy-start(s32[64]{0:T(128)} %param.9) | copy-start | bytes 772
  3.5 27.7 %all-to-all-start = ((bf16[32,8,1280]{2,0,1:T(8,128)(2,1)}), bf16[32,8,1280]{2,0,1:T(8,128)(2,1)S(1)}, u32[]{:S(2)}, u32[]{:S(2)}) async-start(bf16[32,8,1280]{2,0,1:T(8,128)(2,1)} %pad_maximum_fusion), calls=%async_computation | async-start | bytes 1310720 | tf_op jit(solution)/shard_map/all_to_all | solution.py:297
  10.5 28.1 %collective-permute-start.1 = (bf16[16,128,256]{2,1,0:T(8,128)(2,1)S(1)}, bf16[16,128,256]{2,1,0:T(8,128)(2,1)}, u32[]{:S(2)}, u32[]{:S(2)}) collective-permute-start(bf16[16,128,256]{2,1,0:T(8,128)(2,1)S(1)} %bitcast.26), channel_id=1, source_target_pairs={{0,112},{8,24},{16,0},{24,40},{32,16},{40,56},{48,32},{56,72},{64,... | collective-permute-start | bytes 3145736 | tf_op jit(solution)/shard_map/ppermute | solution.py:275
  14.5 31.0 %collective-permute-start = (bf16[16,128,256]{2,1,0:T(8,128)(2,1)S(1)}, bf16[16,128,256]{2,1,0:T(8,128)(2,1)}, u32[]{:S(2)}, u32[]{:S(2)}) collective-permute-start(bf16[16,128,256]{2,1,0:T(8,128)(2,1)S(1)} %bitcast.27), channel_id=1, source_target_pairs={{0,16},{8,120},{16,32},{24,8},{32,48},{40,24},{48,64},{56,40},{64,... | collective-permute-start | bytes 3145736 | tf_op jit(solution)/shard_map/ppermute | solution.py:275
  31.2 0.8 copy-start.3
  32.1 22.3 %all-to-all-start.1 = ((bf16[8,2,128,256]{3,2,1,0:T(8,128)(2,1)}), bf16[8,2,128,256]{3,2,1,0:T(8,128)(2,1)S(1)}, u32[]{:S(2)}, u32[]{:S(2)}) async-start(bf16[8,2,128,256]{3,2,1,0:T(8,128)(2,1)} %shard_map.64), calls=%async_computation.1 | async-start | bytes 2097152 | tf_op jit(solution)/shard_map/all_to_all | solution.py:278
  38.6 33.0 %collective-permute-start.3 = (bf16[16,128,256]{2,1,0:T(8,128)(2,1)}, bf16[16,128,256]{2,1,0:T(8,128)(2,1)}, u32[]{:S(2)}, u32[]{:S(2)}) collective-permute-start(bf16[16,128,256]{2,1,0:T(8,128)(2,1)} %collective-permute-done.1.refs_1_), channel_id=1, source_target_pairs={{0,112},{8,24},{16,0},{24,40},{32,16},{40,56},{48,32},{56,72},{64,... | collective-permute-start | bytes 3145736 | tf_op jit(solution)/shard_map/ppermute | solution.py:275
  45.5 28.1 %collective-permute-start.2 = (bf16[16,128,256]{2,1,0:T(8,128)(2,1)}, bf16[16,128,256]{2,1,0:T(8,128)(2,1)}, u32[]{:S(2)}, u32[]{:S(2)}) collective-permute-start(bf16[16,128,256]{2,1,0:T(8,128)(2,1)} %collective-permute-done.refs_0_), channel_id=1, source_target_pairs={{0,16},{8,120},{16,32},{24,8},{32,48},{40,24},{48,64},{56,40},{64,... | collective-permute-start | bytes 3145736 | tf_op jit(solution)/shard_map/ppermute | solution.py:275
  54.4 6.7 %copy-start.5 = (s32[64,64]{1,0:T(8,128)S(1)}, s32[64,64]{1,0:T(8,128)}, u32[]{:S(2)}) copy-start(s32[64,64]{1,0:T(8,128)} %select_reduce_fusion.table) | copy-start | bytes 49156
  54.4 6.7 %copy-start.7 = (s32[6]{0:T(128)S(1)}, s32[6]{0:T(128)}, u32[]{:S(2)}) copy-start(s32[6]{0:T(128)} %stack.15.place) | copy-start | bytes 76
  54.4 33.6 %all-to-all-start.4 = ((bf16[8,2,128,256]{3,2,1,0:T(8,128)(2,1)}), bf16[8,2,128,256]{3,2,1,0:T(8,128)(2,1)S(1)}, u32[]{:S(2)}, u32[]{:S(2)}) async-start(bf16[8,2,128,256]{3,2,1,0:T(8,128)(2,1)} %shard_map.65.refs_2_), calls=%async_computation.4 | async-start | bytes 2097152 | tf_op jit(solution)/shard_map/all_to_all | solution.py:278
  61.0 1.2 copy-start.1
  62.3 1.1 copy-start.4
  69.8 1.0 copy-start.9
  70.8 0.8 copy-start.15
  77.1 39.0 %collective-permute-start.5 = (bf16[8,1,128,256]{3,2,1,0:T(8,128)(2,1)}, bf16[8,1,128,256]{3,2,1,0:T(8,128)(2,1)}, u32[]{:S(2)}, u32[]{:S(2)}) collective-permute-start(bf16[8,1,128,256]{3,2,1,0:T(8,128)(2,1)} %get-tuple-element.24), channel_id=1, source_target_pairs={{0,112},{8,24},{16,0},{24,40},{32,16},{40,56},{48,32},{56,72},{64,... | collective-permute-start | bytes 1572872 | tf_op jit(solution)/shard_map/ppermute | solution.py:275
  79.1 26.7 %collective-permute-start.4 = (bf16[8,1,128,256]{3,2,1,0:T(8,128)(2,1)}, bf16[8,1,128,256]{3,2,1,0:T(8,128)(2,1)}, u32[]{:S(2)}, u32[]{:S(2)}) collective-permute-start(bf16[8,1,128,256]{3,2,1,0:T(8,128)(2,1)} %get-tuple-element.22.refs_2_), channel_id=1, source_target_pairs={{0,16},{8,120},{16,32},{24,8},{32,48},{40,24},{48,64},{56,40},{64,... | collective-permute-start | bytes 1572872 | tf_op jit(solution)/shard_map/ppermute | solution.py:275
  88.0 5.3 %copy-start.6 = (s32[64,64]{1,0:T(8,128)S(1)}, s32[64,64]{1,0:T(8,128)}, u32[]{:S(2)}) copy-start(s32[64,64]{1,0:T(8,128)} %select_reduce_fusion.table) | copy-start | bytes 49156
  88.0 5.3 %copy-start.8 = (s32[6]{0:T(128)S(1)}, s32[6]{0:T(128)}, u32[]{:S(2)}) copy-start(s32[6]{0:T(128)} %stack.15.place) | copy-start | bytes 76
  88.0 30.3 %all-to-all-start.3 = ((bf16[8,2,128,256]{3,2,1,0:T(8,128)(2,1)}), bf16[8,2,128,256]{3,2,1,0:T(8,128)(2,1)S(1)}, u32[]{:S(2)}, u32[]{:S(2)}) async-start(bf16[8,2,128,256]{3,2,1,0:T(8,128)(2,1)} %shard_map.69.refs_4_), calls=%async_computation.3 | async-start | bytes 2097152 | tf_op jit(solution)/shard_map/all_to_all | solution.py:278
  93.3 1.2 copy-start
  94.6 1.2 copy-start.10
  95.8 1.0 copy-start.16
  105.7 1.2 copy-start.11
  106.9 28.4 %collective-permute-start.7 = (bf16[4,1,128,256]{3,2,1,0:T(8,128)(2,1)}, bf16[4,1,128,256]{3,2,1,0:T(8,128)(2,1)S(1)}, u32[]{:S(2)}, u32[]{:S(2)}) collective-permute-start(bf16[4,1,128,256]{3,2,1,0:T(8,128)(2,1)} %get-tuple-element.31), channel_id=1, source_target_pairs={{0,64},{8,72},{16,80},{24,88},{32,96},{40,104},{48,112},{56,120},{... | collective-permute-start | bytes 786440 | tf_op jit(solution)/shard_map/ppermute | solution.py:275
  108.8 26.5 %collective-permute-start.6 = (bf16[4,1,128,256]{3,2,1,0:T(8,128)(2,1)}, bf16[4,1,128,256]{3,2,1,0:T(8,128)(2,1)}, u32[]{:S(2)}, u32[]{:S(2)}) collective-permute-start(bf16[4,1,128,256]{3,2,1,0:T(8,128)(2,1)} %get-tuple-element.32), channel_id=1, source_target_pairs={{0,64},{8,72},{16,80},{24,88},{32,96},{40,104},{48,112},{56,120},{... | collective-permute-start | bytes 786440 | tf_op jit(solution)/shard_map/ppermute | solution.py:275
  118.3 4.7 %copy-start.2 = (bf16[8,2,128,256]{3,2,1,0:T(8,128)(2,1)S(1)}, bf16[8,2,128,256]{3,2,1,0:T(8,128)(2,1)}, u32[]{:S(2)}) copy-start(bf16[8,2,128,256]{3,2,1,0:T(8,128)(2,1)} %shard_map.68.refs_4_) | copy-start | bytes 3145732
  118.4 18.1 %all-to-all-start.2 = ((bf16[8,2,128,256]{3,2,1,0:T(8,128)(2,1)}), bf16[8,2,128,256]{3,2,1,0:T(8,128)(2,1)S(1)}, u32[]{:S(2)}, u32[]{:S(2)}) async-start(bf16[8,2,128,256]{3,2,1,0:T(8,128)(2,1)} %shard_map.68.refs_4_), calls=%async_computation.2 | async-start | bytes 2097152 | tf_op jit(solution)/shard_map/all_to_all | solution.py:278
  123.0 1.2 copy-start.12
  124.3 1.0 copy-start.17
  134.4 1.0 copy-start.13
  136.4 1.2 copy-start.14
  137.7 1.0 copy-start.18

commit v3 on v2

--- a/solution.py
+++ b/solution.py
@@ -309,15 +309,18 @@
     (send_near,) = get([long1, short1], (((0, 0, -1), (1, 0, 1)),))
     near = deliver(send_near)
     *state, query = step(q_kv, [start], ((0, (None, 0)),), None, False, after=[send_near])
-    send_long, send_short = get([long2, short2], (((0, 1, -2),), ((1, -1, 2),)), after=[state[0]])
+    send_long, send_short, middle_sent = get(
+        [long2, short2],
+        (((0, 1, -2),), ((1, -1, 2),), ((0, 0, -2), (1, 0, 2))),
+        after=[state[0]],
+        cost=40,
+    )
+    far, _ = lax.optimization_barrier((start, near))
     long3, short3 = hop(send_long, 1, True), hop(send_short, -1, True)
-    (middle_sent,) = get([long2, short2], (((0, 0, -2), (1, 0, 2)),), after=[send_long])
     middle = deliver(middle_sent)
-    state = step(query, [near], ((0, (-1, 1)),), state, False, after=[middle_sent])
-    far, long3 = lax.optimization_barrier((start, long3))
     far_up, far_down = hop(far[:half_peers, :1], 4, False), hop(far[half_peers:, :1], -4, False)
-    third = join([long3, short3], cost=30)
-    state = step(query, [middle], ((0, (-2, 2)),), state, False, after=[third], cost=10)
+    third = join([long3, short3], cost=4)
+    state = step(query, [near, middle], ((0, (-1, 1)), (0, (-2, 2))), state, False, after=[third], cost=60)
     third = deliver(third)
     (attended,) = step(
         query, [third, far_up, far_down], ((0, (-3, 3)), (0, (4,)), (half_peers, (4,))), state, True

time: 177 us -> 166 us (0.938)
  the two profiles are of different devices: /device:TPU:7 before, /device:TPU:194 now
where the time goes in v3:
time: 166 us; the launch traced here: 165 us
  starting transfers between devices  60.4 us (36%)
  Pallas kernels  45 us (27%)
  blocking collectives  29 us (17%)
  local copies, waits for them, and re-layouts  13.4 us (8%)
  waiting for transfers between devices  13.3 us (8%)
  other arithmetic  3.29 us (2%)
    ppermute x8, starting transfers between devices, hop(): return lax.ppermute(array, ('z', 'core'), pairs)  32.3 us
    pallas_call x3, Pallas kernels, attend(): pl.pallas_call(functools.partial(attend_kernel, rounds, chunk, first, las...  31.3 us
    all_to_all x1, blocking collectives, local(): lax.all_to_all(attended, 'tp', split_axis=0, concat_axis=2, tiled=True)  29 us
    all_to_all x4, starting transfers between devices, deliver(): return lax.all_to_all(array, PLANE, split_axis=0, concat_axis=0, tiled=True)  20.9 us
    pallas_call x3, Pallas kernels, pick(): pl.pallas_call(functools.partial(pick_kernel, outputs, len(buffers)), gri...  11.5 us
    unnamed x42, local copies, waits for them, and re-layouts  10.7 us
    all_to_all x1, starting transfers between devices, local(): q_kv = lax.all_to_all(both, 'tp', split_axis=1, concat_axis=0, tiled=True)  7.23 us
    ppermute x8, waiting for transfers between devices, hop(): return lax.ppermute(array, ('z', 'core'), pairs)  5.97 us
  transfers between devices with their start and end apart: 13, of which 5 were waited for; matrix products, arithmetic and copies ran while one was open for 2% of the time, Pallas kernels for 20%

profile of v3, /device:TPU:194, one launch (start us, length us, event | category | flops | bytes accessed | tf_op | source)
XLA Modules:
  0.0 164.9 jit_solution(6035991487802833123)
XLA Ops:
  0.0 1.4 copy.18
  1.4 0.3 copy.14
  1.7 0.0 copy-done.15
  1.7 0.0 copy-start.19
  1.7 0.0 copy-start.17
  1.7 0.0 copy-start.16
  1.8 0.9 pad_maximum_fusion
  2.6 7.2 %all-to-all-start = ((bf16[32,8,1280]{2,0,1:T(8,128)(2,1)}), bf16[32,8,1280]{2,0,1:T(8,128)(2,1)S(1)}, u32[]{:S(2)}, u32[]{:S(2)}) async-start(bf16[32,8,1280]{2,0,1:T(8,128)(2,1)} %pad_maximum_fusion), calls=%async_computation | async-start | bytes 1310720 | tf_op jit(solution)/shard_map/all_to_all | solution.py:297
  9.9 0.0 copy-done.19
  9.9 5.5 %collective-permute-start = (bf16[16,128,256]{2,1,0:T(8,128)(2,1)S(1)}, bf16[16,128,256]{2,1,0:T(8,128)(2,1)}, u32[]{:S(2)}, u32[]{:S(2)}) collective-permute-start(bf16[16,128,256]{2,1,0:T(8,128)(2,1)S(1)} %bitcast.26), channel_id=1, source_target_pairs={{0,16},{8,120},{16,32},{24,8},{32,48},{40,24},{48,64},{56,40},{64,... | collective-permute-start | bytes 3145736 | tf_op jit(solution)/shard_map/ppermute | solution.py:275
  15.4 1.9 %collective-permute-start.1 = (bf16[16,128,256]{2,1,0:T(8,128)(2,1)S(1)}, bf16[16,128,256]{2,1,0:T(8,128)(2,1)}, u32[]{:S(2)}, u32[]{:S(2)}) collective-permute-start(bf16[16,128,256]{2,1,0:T(8,128)(2,1)S(1)} %bitcast.27), channel_id=1, source_target_pairs={{0,112},{8,24},{16,0},{24,40},{32,16},{40,56},{48,32},{56,72},{64,... | collective-permute-start | bytes 3145736 | tf_op jit(solution)/shard_map/ppermute | solution.py:275
  17.3 0.0 copy-done.17
  17.3 0.1 copy.13
  17.4 0.0 copy-done.16
  17.4 0.1 copy.12
  17.5 0.6 stack.15.place
  18.1 0.0 copy-done.18
  18.1 0.1 iota_compare_fusion.1
  18.2 2.3 %select_reduce_fusion.table = s32[64,64]{1,0:T(8,128)} fusion(s32[64,48]{1,0:T(8,128)S(1)} %copy.13, s32[64,48]{1,0:T(8,128)S(1)} %copy.12, pred[64,48]{1,0:T(8,128)(4,1)S(1)} %iota_compare_fusion.1), kind=kLoop, calls=%fused_computation | loop fusion | flops 782336 | bytes 44032 | tf_op jit(solution)/shard_map/reduce_sum | solution.py:287
  20.5 3.7 %shard_map.64 = bf16[8,2,128,256]{3,2,1,0:T(8,128)(2,1)} custom-call(s32[6]{0:T(128)} %stack.15.place, s32[64,64]{1,0:T(8,128)} %select_reduce_fusion.table, bf16[16,128,256]{2,1,0:T(8,128)(2,1)} %bitcast.25), custom_call_target="tpu_custom_call" | custom-call | flops 4400000000 | bytes 14400000 | tf_op jit(solution)/shard_map/pallas_call | solution.py:54
  24.3 5.9 %all-to-all-done = bf16[32,8,1280]{2,0,1:T(8,128)(2,1)S(1)} async-done(((bf16[32,8,1280]{2,0,1:T(8,128)(2,1)}), bf16[32,8,1280]{2,0,1:T(8,128)(2,1)S(1)}, u32[]{:S(2)}, u32[]{:S(2)}) %all-to-all-start) | async-done | bytes 655392 | tf_op jit(solution)/shard_map/all_to_all | solution.py:297
  30.2 0.8 copy-done.2
  31.0 4.8 %all-to-all-start.1 = ((bf16[8,2,128,256]{3,2,1,0:T(8,128)(2,1)}), bf16[8,2,128,256]{3,2,1,0:T(8,128)(2,1)S(1)}, u32[]{:S(2)}, u32[]{:S(2)}) async-start(bf16[8,2,128,256]{3,2,1,0:T(8,128)(2,1)} %shard_map.64), calls=%async_computation.1 | async-start | bytes 2097152 | tf_op jit(solution)/shard_map/all_to_all | solution.py:278
  35.9 2.6 %collective-permute-done.refs_0_ = bf16[16,128,256]{2,1,0:T(8,128)(2,1)} collective-permute-done((bf16[16,128,256]{2,1,0:T(8,128)(2,1)S(1)}, bf16[16,128,256]{2,1,0:T(8,128)(2,1)}, u32[]{:S(2)}, u32[]{:S(2)}) %collective-permute-start) | collective-permute-done | bytes 1048608 | tf_op jit(solution)/shard_map/ppermute | solution.py:275
  38.5 5.7 %collective-permute-start.2 = (bf16[16,128,256]{2,1,0:T(8,128)(2,1)}, bf16[16,128,256]{2,1,0:T(8,128)(2,1)}, u32[]{:S(2)}, u32[]{:S(2)}) collective-permute-start(bf16[16,128,256]{2,1,0:T(8,128)(2,1)} %collective-permute-done.refs_0_), channel_id=1, source_target_pairs={{0,16},{8,120},{16,32},{24,8},{32,48},{40,24},{48,64},{56,40},{64,... | collective-permute-start | bytes 3145736 | tf_op jit(solution)/shard_map/ppermute | solution.py:275
  44.2 0.0 collective-permute-done.1.refs_1_
  44.2 1.9 %collective-permute-start.3 = (bf16[16,128,256]{2,1,0:T(8,128)(2,1)}, bf16[16,128,256]{2,1,0:T(8,128)(2,1)}, u32[]{:S(2)}, u32[]{:S(2)}) collective-permute-start(bf16[16,128,256]{2,1,0:T(8,128)(2,1)} %collective-permute-done.1.refs_1_), channel_id=1, source_target_pairs={{0,112},{8,24},{16,0},{24,40},{32,16},{40,56},{48,32},{56,72},{64,... | collective-permute-start | bytes 3145736 | tf_op jit(solution)/shard_map/ppermute | solution.py:275
  46.1 3.5 %shard_map.65.refs_2_ = bf16[8,2,128,256]{3,2,1,0:T(8,128)(2,1)} custom-call(s32[6]{0:T(128)} %stack.15.place, s32[64,64]{1,0:T(8,128)} %select_reduce_fusion.table, bf16[16,128,256]{2,1,0:T(8,128)(2,1)} %collective-permute-done.refs_0_, bf16[16,128,256]{2,1,0:T(8,128)(2,1)} %collective-permute-done.1.refs_1_), custom_call_target="tpu_custom_call" | custom-call | flops 4400000000 | bytes 14400000 | tf_op jit(solution)/shard_map/pallas_call | solution.py:54
  49.6 0.0 copy-start
  49.6 0.3 all-to-all-done.1.refs_1_
  49.9 4.8 %all-to-all-start.3 = ((bf16[8,2,128,256]{3,2,1,0:T(8,128)(2,1)}), bf16[8,2,128,256]{3,2,1,0:T(8,128)(2,1)S(1)}, u32[]{:S(2)}, u32[]{:S(2)}) async-start(bf16[8,2,128,256]{3,2,1,0:T(8,128)(2,1)} %shard_map.65.refs_2_), calls=%async_computation.3 | async-start | bytes 2097152 | tf_op jit(solution)/shard_map/all_to_all | solution.py:278
  54.7 0.0 copy-done.4
  54.7 1.1 copy-done.3
  55.8 6.4 %shard_map.66 = (f32[8,128,256]{2,1,0:T(8,128)S(1)}, f32[2,8,256]{2,1,0:T(8,128)S(1)}, bf16[1024,256]{1,0:T(8,128)(2,1)S(1)}) custom-call(s32[6]{0:T(128)S(1)} %copy-done.6, s32[64,64]{1,0:T(8,128)S(1)} %copy-done.4, bf16[256,1280]{1,0:T(8,128)(2,1)S(1)} %bitcast.19, bf16[8,2,128,256]{3,2,1,0:T(8,128)(2,1)S(1)} %all-to-all-done.1.refs_1_, ...), custom_call_target="tpu_custom_call" | custom-call | flops 8800000000 | bytes 28800000 | tf_op jit(solution)/shard_map/pallas_call | solution.py:231
  62.2 0.0 copy-start.10
  62.2 1.0 copy-done.10
  63.2 0.8 copy-done.12
  64.0 3.4 %collective-permute-done.2.refs_0_ = bf16[16,128,256]{2,1,0:T(8,128)(2,1)} collective-permute-done((bf16[16,128,256]{2,1,0:T(8,128)(2,1)}, bf16[16,128,256]{2,1,0:T(8,128)(2,1)}, u32[]{:S(2)}, u32[]{:S(2)}) %collective-permute-start.2) | collective-permute-done | bytes 1048608 | tf_op jit(solution)/shard_map/ppermute | solution.py:275
  67.3 0.0 collective-permute-done.3.refs_1_
  67.3 4.3 %shard_map.67 = (bf16[8,1,128,256]{3,2,1,0:T(8,128)(2,1)}, bf16[8,1,128,256]{3,2,1,0:T(8,128)(2,1)}, bf16[8,2,128,256]{3,2,1,0:T(8,128)(2,1)}) custom-call(s32[6]{0:T(128)} %stack.15.place, s32[64,64]{1,0:T(8,128)} %select_reduce_fusion.table, bf16[16,128,256]{2,1,0:T(8,128)(2,1)} %collective-permute-done.2.refs_0_, ...), custom_call_target="tpu_custom_call" | custom-call | flops 44000002048 | bytes 144000000 | tf_op jit(solution)/shard_map/pallas_call | solution.py:54
  71.6 5.6 %collective-permute-start.4 = (bf16[8,1,128,256]{3,2,1,0:T(8,128)(2,1)}, bf16[8,1,128,256]{3,2,1,0:T(8,128)(2,1)}, u32[]{:S(2)}, u32[]{:S(2)}) collective-permute-start(bf16[8,1,128,256]{3,2,1,0:T(8,128)(2,1)} %get-tuple-element.20), channel_id=1, source_target_pairs={{0,16},{8,120},{16,32},{24,8},{32,48},{40,24},{48,64},{56,40},{64,... | collective-permute-start | bytes 1572872 | tf_op jit(solution)/shard_map/ppermute | solution.py:275
  77.2 1.9 %collective-permute-start.5 = (bf16[8,1,128,256]{3,2,1,0:T(8,128)(2,1)}, bf16[8,1,128,256]{3,2,1,0:T(8,128)(2,1)}, u32[]{:S(2)}, u32[]{:S(2)}) collective-permute-start(bf16[8,1,128,256]{3,2,1,0:T(8,128)(2,1)} %get-tuple-element.21), channel_id=1, source_target_pairs={{0,112},{8,24},{16,0},{24,40},{32,16},{40,56},{48,32},{56,72},{64,... | collective-permute-start | bytes 1572872 | tf_op jit(solution)/shard_map/ppermute | solution.py:275
  79.2 0.0 all-to-all-done.3.refs_1_
  79.2 5.1 %all-to-all-start.4 = ((bf16[8,2,128,256]{3,2,1,0:T(8,128)(2,1)}), bf16[8,2,128,256]{3,2,1,0:T(8,128)(2,1)S(1)}, u32[]{:S(2)}, u32[]{:S(2)}) async-start(bf16[8,2,128,256]{3,2,1,0:T(8,128)(2,1)} %get-tuple-element.23), calls=%async_computation.4 | async-start | bytes 2097152 | tf_op jit(solution)/shard_map/all_to_all | solution.py:278
  84.3 0.8 fusion.1
  85.1 4.6 %collective-permute-start.6 = (bf16[4,1,128,256]{3,2,1,0:T(8,128)(2,1)}, bf16[4,1,128,256]{3,2,1,0:T(8,128)(2,1)S(1)}, u32[]{:S(2)}, u32[]{:S(2)}) collective-permute-start(bf16[4,1,128,256]{3,2,1,0:T(8,128)(2,1)} %get-tuple-element.28), channel_id=1, source_target_pairs={{0,64},{8,72},{16,80},{24,88},{32,96},{40,104},{48,112},{56,120},{... | collective-permute-start | bytes 786440 | tf_op jit(solution)/shard_map/ppermute | solution.py:275
  89.8 5.1 %collective-permute-start.7 = (bf16[4,1,128,256]{3,2,1,0:T(8,128)(2,1)}, bf16[4,1,128,256]{3,2,1,0:T(8,128)(2,1)}, u32[]{:S(2)}, u32[]{:S(2)}) collective-permute-start(bf16[4,1,128,256]{3,2,1,0:T(8,128)(2,1)} %get-tuple-element.27), channel_id=1, source_target_pairs={{0,64},{8,72},{16,80},{24,88},{32,96},{40,104},{48,112},{56,120},{... | collective-permute-start | bytes 786440 | tf_op jit(solution)/shard_map/ppermute | solution.py:275
  94.9 0.0 collective-permute-done.4.refs_0_
  94.9 0.0 collective-permute-done.5.refs_1_
  94.9 2.2 %shard_map.68.refs_5_ = bf16[8,2,128,256]{3,2,1,0:T(8,128)(2,1)} custom-call(bf16[8,1,128,256]{3,2,1,0:T(8,128)(2,1)} %collective-permute-done.4.refs_0_, bf16[8,1,128,256]{3,2,1,0:T(8,128)(2,1)} %collective-permute-done.5.refs_1_), custom_call_target="tpu_custom_call" | custom-call | flops 4400000000 | bytes 14400000 | tf_op jit(solution)/shard_map/pallas_call | solution.py:80
  97.1 1.2 all-to-all-done.4.refs_2_
  98.3 6.2 %all-to-all-start.2 = ((bf16[8,2,128,256]{3,2,1,0:T(8,128)(2,1)}), bf16[8,2,128,256]{3,2,1,0:T(8,128)(2,1)}, u32[]{:S(2)}, u32[]{:S(2)}) async-start(bf16[8,2,128,256]{3,2,1,0:T(8,128)(2,1)} %shard_map.68.refs_5_), calls=%async_computation.2 | async-start | bytes 2097152 | tf_op jit(solution)/shard_map/all_to_all | solution.py:278
  104.5 1.2 copy-done.1
  105.8 1.0 copy-done.13
  106.8 12.9 %shard_map.69 = (f32[8,128,256]{2,1,0:T(8,128)S(1)}, f32[2,8,256]{2,1,0:T(8,128)S(1)}) custom-call(s32[6]{0:T(128)S(1)} %copy-done.7, s32[64,64]{1,0:T(8,128)S(1)} %copy-done.5, bf16[1024,256]{1,0:T(8,128)(2,1)S(1)} %copy-done.13, bf16[8,2,128,256]{3,2,1,0:T(8,128)(2,1)S(1)} %all-to-all-done.3.refs_1_, bf16[8,2,128,256]{3,2,1,0:T(8,128)(2,1)S(1)} %all-to-all-done.4.refs_2_, ...), custom_call_target="tpu_custom_call" | custom-call | flops 65999998976 | bytes 216000000 | tf_op jit(solution)/shard_map/pallas_call | solution.py:231
  119.7 1.0 copy-done.8
  120.7 0.0 collective-permute-done.6.refs_2_
  120.7 0.0 collective-permute-done.7.refs_3_
  120.7 0.0 all-to-all-done.2.refs_1_
  120.7 1.2 copy-done.9
  121.9 1.0 copy-done.14
  123.0 12.0 %shard_map.70 = bf16[256,1024]{1,0:T(8,128)(2,1)S(1)} custom-call(s32[6]{0:T(128)S(1)} %copy-done.7, s32[64,64]{1,0:T(8,128)S(1)} %copy-done.5, bf16[1024,256]{1,0:T(8,128)(2,1)S(1)} %copy-done.14, bf16[8,2,128,256]{3,2,1,0:T(8,128)(2,1)} %all-to-all-done.2.refs_1_, bf16[4,1,128,256]{3,2,1,0:T(8,128)(2,1)S(1)} %collective-permute-done.6.refs_2_, ...), custom_call_target="tpu_custom_call" | custom-call | flops 8800000000 | bytes 28800000 | tf_op jit(solution)/shard_map/pallas_call | solution.py:231
  135.0 29.0 %all_to_all.53 = bf16[8,32,1024]{2,1,0:T(8,128)(2,1)S(1)} all-to-all(bf16[8,32,1024]{2,1,0:T(8,128)(2,1)S(1)} %bitcast.20), channel_id=1, replica_groups=mesh['pool'=4,'z'=8,'core'=2,'tp'=8] {'tp'}, dimensions={0} | all-to-all | bytes 1048576 | tf_op jit(solution)/shard_map/all_to_all | solution.py:329
  164.0 0.8 copy.17
  (22 shorter events, 0.1 us)
Async XLA Ops:
  0.0 1.7 %copy-start.15 = (bf16[1,32,8,256]{3,2,1,0:T(8,128)(2,1)S(1)}, bf16[1,32,8,256]{3,2,1,0:T(8,128)(2,1)}, u32[]{:S(2)}) copy-start(bf16[1,32,8,256]{3,2,1,0:T(8,128)(2,1)} %param.7) | copy-start | bytes 393220
  1.7 8.2 %copy-start.19 = (bf16[16,128,1,256]{3,1,2,0:T(8,128)(2,1)S(1)}, bf16[16,128,1,256]{3,1,2,0:T(8,128)(2,1)}, u32[]{:S(2)}) copy-start(bf16[16,128,1,256]{3,1,2,0:T(8,128)(2,1)} %param.8) | copy-start | bytes 3145732
  1.7 15.6 %copy-start.17 = (s32[64,48]{0,1:T(8,128)S(1)}, s32[64,48]{0,1:T(8,128)}, u32[]{:S(2)}) copy-start(s32[64,48]{0,1:T(8,128)} %param.11) | copy-start | bytes 36868
  1.7 15.7 %copy-start.16 = (s32[64,48]{0,1:T(8,128)S(1)}, s32[64,48]{0,1:T(8,128)}, u32[]{:S(2)}) copy-start(s32[64,48]{0,1:T(8,128)} %param.10) | copy-start | bytes 36868
  2.6 15.5 %copy-start.18 = (s32[64]{0:T(128)S(1)}, s32[64]{0:T(128)}, u32[]{:S(2)}) copy-start(s32[64]{0:T(128)} %param.9) | copy-start | bytes 772
  2.6 27.5 %all-to-all-start = ((bf16[32,8,1280]{2,0,1:T(8,128)(2,1)}), bf16[32,8,1280]{2,0,1:T(8,128)(2,1)S(1)}, u32[]{:S(2)}, u32[]{:S(2)}) async-start(bf16[32,8,1280]{2,0,1:T(8,128)(2,1)} %pad_maximum_fusion), calls=%async_computation | async-start | bytes 1310720 | tf_op jit(solution)/shard_map/all_to_all | solution.py:297
  9.9 28.6 %collective-permute-start = (bf16[16,128,256]{2,1,0:T(8,128)(2,1)S(1)}, bf16[16,128,256]{2,1,0:T(8,128)(2,1)}, u32[]{:S(2)}, u32[]{:S(2)}) collective-permute-start(bf16[16,128,256]{2,1,0:T(8,128)(2,1)S(1)} %bitcast.26), channel_id=1, source_target_pairs={{0,16},{8,120},{16,32},{24,8},{32,48},{40,24},{48,64},{56,40},{64,... | collective-permute-start | bytes 3145736 | tf_op jit(solution)/shard_map/ppermute | solution.py:275
  15.4 28.8 %collective-permute-start.1 = (bf16[16,128,256]{2,1,0:T(8,128)(2,1)S(1)}, bf16[16,128,256]{2,1,0:T(8,128)(2,1)}, u32[]{:S(2)}, u32[]{:S(2)}) collective-permute-start(bf16[16,128,256]{2,1,0:T(8,128)(2,1)S(1)} %bitcast.27), channel_id=1, source_target_pairs={{0,112},{8,24},{16,0},{24,40},{32,16},{40,56},{48,32},{56,72},{64,... | collective-permute-start | bytes 3145736 | tf_op jit(solution)/shard_map/ppermute | solution.py:275
  30.2 0.9 copy-start.2
  31.0 18.9 %all-to-all-start.1 = ((bf16[8,2,128,256]{3,2,1,0:T(8,128)(2,1)}), bf16[8,2,128,256]{3,2,1,0:T(8,128)(2,1)S(1)}, u32[]{:S(2)}, u32[]{:S(2)}) async-start(bf16[8,2,128,256]{3,2,1,0:T(8,128)(2,1)} %shard_map.64), calls=%async_computation.1 | async-start | bytes 2097152 | tf_op jit(solution)/shard_map/all_to_all | solution.py:278
  38.5 28.8 %collective-permute-start.2 = (bf16[16,128,256]{2,1,0:T(8,128)(2,1)}, bf16[16,128,256]{2,1,0:T(8,128)(2,1)}, u32[]{:S(2)}, u32[]{:S(2)}) collective-permute-start(bf16[16,128,256]{2,1,0:T(8,128)(2,1)} %collective-permute-done.refs_0_), channel_id=1, source_target_pairs={{0,16},{8,120},{16,32},{24,8},{32,48},{40,24},{48,64},{56,40},{64,... | collective-permute-start | bytes 3145736 | tf_op jit(solution)/shard_map/ppermute | solution.py:275
  44.2 23.1 %collective-permute-start.3 = (bf16[16,128,256]{2,1,0:T(8,128)(2,1)}, bf16[16,128,256]{2,1,0:T(8,128)(2,1)}, u32[]{:S(2)}, u32[]{:S(2)}) collective-permute-start(bf16[16,128,256]{2,1,0:T(8,128)(2,1)} %collective-permute-done.1.refs_1_), channel_id=1, source_target_pairs={{0,112},{8,24},{16,0},{24,40},{32,16},{40,56},{48,32},{56,72},{64,... | collective-permute-start | bytes 3145736 | tf_op jit(solution)/shard_map/ppermute | solution.py:275
  49.6 5.1 %copy-start = (bf16[8,2,128,256]{3,2,1,0:T(8,128)(2,1)S(1)}, bf16[8,2,128,256]{3,2,1,0:T(8,128)(2,1)}, u32[]{:S(2)}) copy-start(bf16[8,2,128,256]{3,2,1,0:T(8,128)(2,1)} %shard_map.65.refs_2_) | copy-start | bytes 3145732
  49.6 5.1 %copy-start.4 = (s32[64,64]{1,0:T(8,128)S(1)}, s32[64,64]{1,0:T(8,128)}, u32[]{:S(2)}) copy-start(s32[64,64]{1,0:T(8,128)} %select_reduce_fusion.table) | copy-start | bytes 49156
  49.6 5.1 %copy-start.6 = (s32[6]{0:T(128)S(1)}, s32[6]{0:T(128)}, u32[]{:S(2)}) copy-start(s32[6]{0:T(128)} %stack.15.place) | copy-start | bytes 76
  49.9 29.3 %all-to-all-start.3 = ((bf16[8,2,128,256]{3,2,1,0:T(8,128)(2,1)}), bf16[8,2,128,256]{3,2,1,0:T(8,128)(2,1)S(1)}, u32[]{:S(2)}, u32[]{:S(2)}) async-start(bf16[8,2,128,256]{3,2,1,0:T(8,128)(2,1)} %shard_map.65.refs_2_), calls=%async_computation.3 | async-start | bytes 2097152 | tf_op jit(solution)/shard_map/all_to_all | solution.py:278
  54.7 1.1 copy-start.3
  62.2 1.0 copy-start.10
  63.2 0.8 copy-start.12
  71.6 23.3 %collective-permute-start.4 = (bf16[8,1,128,256]{3,2,1,0:T(8,128)(2,1)}, bf16[8,1,128,256]{3,2,1,0:T(8,128)(2,1)}, u32[]{:S(2)}, u32[]{:S(2)}) collective-permute-start(bf16[8,1,128,256]{3,2,1,0:T(8,128)(2,1)} %get-tuple-element.20), channel_id=1, source_target_pairs={{0,16},{8,120},{16,32},{24,8},{32,48},{40,24},{48,64},{56,40},{64,... | collective-permute-start | bytes 1572872 | tf_op jit(solution)/shard_map/ppermute | solution.py:275
  77.2 17.7 %collective-permute-start.5 = (bf16[8,1,128,256]{3,2,1,0:T(8,128)(2,1)}, bf16[8,1,128,256]{3,2,1,0:T(8,128)(2,1)}, u32[]{:S(2)}, u32[]{:S(2)}) collective-permute-start(bf16[8,1,128,256]{3,2,1,0:T(8,128)(2,1)} %get-tuple-element.21), channel_id=1, source_target_pairs={{0,112},{8,24},{16,0},{24,40},{32,16},{40,56},{48,32},{56,72},{64,... | collective-permute-start | bytes 1572872 | tf_op jit(solution)/shard_map/ppermute | solution.py:275
  79.2 19.2 %all-to-all-start.4 = ((bf16[8,2,128,256]{3,2,1,0:T(8,128)(2,1)}), bf16[8,2,128,256]{3,2,1,0:T(8,128)(2,1)S(1)}, u32[]{:S(2)}, u32[]{:S(2)}) async-start(bf16[8,2,128,256]{3,2,1,0:T(8,128)(2,1)} %get-tuple-element.23), calls=%async_computation.4 | async-start | bytes 2097152 | tf_op jit(solution)/shard_map/all_to_all | solution.py:278
  85.1 35.6 %collective-permute-start.6 = (bf16[4,1,128,256]{3,2,1,0:T(8,128)(2,1)}, bf16[4,1,128,256]{3,2,1,0:T(8,128)(2,1)S(1)}, u32[]{:S(2)}, u32[]{:S(2)}) collective-permute-start(bf16[4,1,128,256]{3,2,1,0:T(8,128)(2,1)} %get-tuple-element.28), channel_id=1, source_target_pairs={{0,64},{8,72},{16,80},{24,88},{32,96},{40,104},{48,112},{56,120},{... | collective-permute-start | bytes 786440 | tf_op jit(solution)/shard_map/ppermute | solution.py:275
  89.8 30.9 %collective-permute-start.7 = (bf16[4,1,128,256]{3,2,1,0:T(8,128)(2,1)}, bf16[4,1,128,256]{3,2,1,0:T(8,128)(2,1)}, u32[]{:S(2)}, u32[]{:S(2)}) collective-permute-start(bf16[4,1,128,256]{3,2,1,0:T(8,128)(2,1)} %get-tuple-element.27), channel_id=1, source_target_pairs={{0,64},{8,72},{16,80},{24,88},{32,96},{40,104},{48,112},{56,120},{... | collective-permute-start | bytes 786440 | tf_op jit(solution)/shard_map/ppermute | solution.py:275
  97.1 7.4 %copy-start.5 = (s32[64,64]{1,0:T(8,128)S(1)}, s32[64,64]{1,0:T(8,128)}, u32[]{:S(2)}) copy-start(s32[64,64]{1,0:T(8,128)} %select_reduce_fusion.table) | copy-start | bytes 49156
  97.1 7.4 %copy-start.7 = (s32[6]{0:T(128)S(1)}, s32[6]{0:T(128)}, u32[]{:S(2)}) copy-start(s32[6]{0:T(128)} %stack.15.place) | copy-start | bytes 76
  97.1 7.4 %copy-start.11 = (f32[8,128,256]{2,1,0:T(8,128)S(1)}, f32[8,128,256]{2,1,0:T(8,128)}, u32[]{:S(2)}) copy-start(f32[8,128,256]{2,1,0:T(8,128)} %copy-done.10) | copy-start | bytes 3145732
  98.3 22.4 %all-to-all-start.2 = ((bf16[8,2,128,256]{3,2,1,0:T(8,128)(2,1)}), bf16[8,2,128,256]{3,2,1,0:T(8,128)(2,1)}, u32[]{:S(2)}, u32[]{:S(2)}) async-start(bf16[8,2,128,256]{3,2,1,0:T(8,128)(2,1)} %shard_map.68.refs_5_), calls=%async_computation.2 | async-start | bytes 2097152 | tf_op jit(solution)/shard_map/all_to_all | solution.py:278
  104.5 1.2 copy-start.1
  105.8 1.0 copy-start.13
  119.7 1.0 copy-start.8
  120.7 1.2 copy-start.9
  121.9 1.0 copy-start.14
